TPU v7x, 256 devices: a whole 4x4x8 slice. The times are simulated.
256 devices in a mesh: seq: 32 (over z, y), head: 8 (over x, core).
Axes of the slice: x: 4, y: 4, z: 8, core: 2. Of those that a mesh axis runs over, the one named last changes fastest.
Arguments:
- ssm_input: bfloat16 [8192, 8192], P('seq', 'head'), may hold values from -0.59765625 to 0.59765625
- ssm_grad_out: bfloat16 [8192, 8192], P('seq', 'head'), may hold values from -6 to 6
- write_coef: bfloat16 [8192, 128], P('seq'), may hold values from -0.059814453 to 0.059814453
- read_coef: bfloat16 [8192, 128], P('seq'), may hold values from -0.059814453 to 0.059814453
- step_size: float32 [64, 8192], P('head', 'seq'), may hold values from 0.25 to 4
- decay_rate: float32 [64], P('head'), may hold values from 5e-05 to 0.1
- skip_gain: float32 [64], P('head'), may hold values from 0.5 to 1.5
- queries: bfloat16 [8192, 4096], P('seq', 'head'), may hold values from -8 to 8
- att_keys: bfloat16 [8192, 1024], P('seq', 'head'), may hold values from -8 to 8
- att_values: bfloat16 [8192, 1024], P('seq', 'head'), may hold values from -6 to 6
- out_grad: bfloat16 [8192, 4096], P('seq', 'head'), may hold values from -6 to 6
- doc_lengths: int32 [128], replicated, may hold values from 1 to 1024, 8192 in all
Outputs:
- grad_input: bfloat16 [8192, 8192], P('seq', 'head')
- grad_write: float32 [8192, 128], P(('seq', 'head'))
- grad_read: float32 [8192, 128], P(('seq', 'head'))
- grad_query: bfloat16 [8192, 4096], P('seq', 'head')
- grad_key: bfloat16 [8192, 1024], P('seq', 'head')
- grad_value: bfloat16 [8192, 1024], P('seq', 'head')
Inputs may be any that keep to these rules, and one draw needn't show every extreme that they name: `doc_lengths`: they sum to 8192; the longest document has exactly 1024 tokens.
All inputs are finite; a program needn't handle non-finite values.
Results may differ from a plain program's by a relative error of at most 0.0085.
Values may be sent and summed in bfloat16 or wider, within the bound.
A program may use at most 128 MiB of HBM per device.

v0:
```python
from functools import reduce

import jax
import jax.numpy as jnp
from jax import lax
from jax.sharding import PartitionSpec as P

HEAD_DIM = 128
REACH = 4


neg_fill = -1e30


def carried_in(value, axis, join, neutral, backward):
    count, mine = (lax.axis_size(axis), lax.axis_index(axis))
    pieces = jax.tree.map(lambda part: lax.all_gather(part, axis), value)
    if backward:
        pieces = jax.tree.map(lambda part: part[::-1], pieces)
        mine = count - 1 - mine
    running = jax.tree.map(
        lambda part, zero: jnp.full_like(part, 0) + jnp.asarray(zero, part.dtype), value, neutral
    )

    def lap(position, running):
        longer = join(running, jax.tree.map(lambda part: part[position], pieces))
        return jax.tree.map(lambda new, old: jnp.where(position < mine, new, old), longer, running)

    return lax.fori_loop(0, count - 1, lap, running)


def shifted(block, axis, distance):
    devices = range(lax.axis_size(axis))
    route = [(i - distance, i) for i in devices if i - distance in devices]
    return lax.ppermute(block, axis, route)


def chain_combine(earlier, latter):
    return (earlier[0] * latter[0], latter[0][:, None, None] * earlier[1] + latter[1])


def doc_starts(doc_lengths, element_indices):
    doc_ends = jnp.cumsum(doc_lengths, dtype=jnp.int32)
    doc_first = doc_ends - doc_lengths
    chosen = jnp.where(
        doc_first[None, :] <= element_indices[:, None],
        doc_first[None, :],
        jnp.zeros_like(doc_first)[None, :],
    )
    return jnp.max(chosen, axis=1)


def reset_factors(running, first_blk, block_first):
    totals = running[:, -1]
    began_before = first_blk < block_first
    continues = first_blk == first_blk[-1]
    tail_decay = jnp.where(continues[None, :], jnp.exp(totals[:, None] - running), 0.0)
    lead_decay = jnp.where(began_before[None, :], jnp.exp(running), 0.0)
    decay_total = jnp.where(began_before[-1], jnp.exp(totals), jnp.zeros_like(totals))
    return (tail_decay, lead_decay, decay_total)


def block_scores(queries4, keys_blk, key_mask, scale_factor):
    scores = (
        jnp.einsum("tkgd,skd->kgts", queries4, keys_blk, preferred_element_type=jnp.float32)
        * scale_factor
    )
    return jnp.where(key_mask[None, None], scores, neg_fill)


def block_weights(scores, key_mask, row_max):
    return jnp.where(key_mask[None, None], jnp.exp(scores - row_max[..., None]), 0.0)


def block_mix(probs_half, values_blk):
    return jnp.einsum("kgts,skd->tkgd", probs_half, values_blk, preferred_element_type=jnp.float32)


def block_grads(
    queries4, grads4, keys_blk, values_blk, probs, probs_half, delta_cols, scale_factor
):
    dprob = jnp.einsum("tkgd,skd->kgts", grads4, values_blk, preferred_element_type=jnp.float32)
    dscore = (probs * (dprob - delta_cols[..., None])).astype(jnp.bfloat16)
    grad_q = jnp.einsum("kgts,skd->tkgd", dscore, keys_blk, preferred_element_type=jnp.float32)
    grad_k = (
        jnp.einsum("kgts,tkgd->skd", dscore, queries4, preferred_element_type=jnp.float32)
        * scale_factor
    )
    grad_v = jnp.einsum("kgts,tkgd->skd", probs_half, grads4, preferred_element_type=jnp.float32)
    return (grad_q, jnp.stack((grad_k, grad_v)))


def on_device(
    ssm_input,
    ssm_grad_out,
    write_coef,
    read_coef,
    step_size,
    decay_rate,
    skip_gain,
    queries,
    att_keys,
    att_values,
    out_grad,
    doc_lengths,
):
    length = ssm_input.shape[0]
    heads_here = decay_rate.shape[0]
    seq_index = lax.axis_index("seq")
    block_start = seq_index * length
    element_indices = block_start + jnp.arange(length, dtype=jnp.int32)
    first_pos = doc_starts(doc_lengths, element_indices)
    running = jnp.cumsum(-decay_rate[:, None] * step_size, axis=1)
    tail_decay, lead_decay, decay_total = reset_factors(running, first_pos, block_start)
    inputs3 = ssm_input.reshape(length, heads_here, -1)
    grads3 = ssm_grad_out.reshape(length, heads_here, -1)
    write_scaled = (tail_decay[:, :, None] * write_coef.astype(jnp.float32)[None]).astype(
        jnp.bfloat16
    )
    read_scaled = (lead_decay[:, :, None] * read_coef.astype(jnp.float32)[None]).astype(
        jnp.bfloat16
    )
    state_part = jnp.einsum(
        "hsn,shp->hnp", write_scaled, inputs3, preferred_element_type=jnp.float32
    )
    adjoint_part = jnp.einsum(
        "htn,thp->hnp", read_scaled, grads3, preferred_element_type=jnp.float32
    )
    identity_pair = (jnp.ones_like(decay_total), jnp.zeros_like(state_part))
    _, state_in = carried_in((decay_total, state_part), "seq", chain_combine, identity_pair, False)
    _, adjoint_in = carried_in(
        (decay_total, adjoint_part), "seq", chain_combine, identity_pair, True
    )
    lower_tri = (jnp.arange(length)[:, None] >= jnp.arange(length)[None, :]) & (
        first_pos[:, None] == first_pos[None, :]
    )
    spread = running[:, :, None] - running[:, None, :]
    decay_mat = jnp.where(lower_tri[None], jnp.exp(jnp.where(lower_tri[None], spread, 0.0)), 0.0)
    corr_mat = jnp.einsum("thp,shp->hts", grads3, inputs3, preferred_element_type=jnp.float32)
    weight_mat = (corr_mat * decay_mat).astype(jnp.bfloat16)
    cross_mat = jnp.dot(read_coef, write_coef.T, preferred_element_type=jnp.float32)
    mix_mat = (cross_mat[None] * decay_mat).astype(jnp.bfloat16)
    input_local = jnp.einsum("hst,shp->thp", mix_mat, grads3, preferred_element_type=jnp.float32)
    write_local = jnp.einsum(
        "hst,sn->tn", weight_mat, read_coef, preferred_element_type=jnp.float32
    )
    read_local = jnp.einsum(
        "hts,sn->tn", weight_mat, write_coef, preferred_element_type=jnp.float32
    )
    state_half = state_in.astype(jnp.bfloat16)
    adjoint_half = adjoint_in.astype(jnp.bfloat16)
    input_carry = (
        jnp.einsum("tn,hnp->thp", write_coef, adjoint_half, preferred_element_type=jnp.float32)
        * tail_decay.T[:, :, None]
    )
    grad_input = (
        (skip_gain[None, :, None] * grads3 + input_local + input_carry)
        .astype(jnp.bfloat16)
        .reshape(length, -1)
    )
    write_carry = jnp.einsum(
        "thp,hnp->htn", inputs3, adjoint_half, preferred_element_type=jnp.float32
    )
    read_carry = jnp.einsum("thp,hnp->htn", grads3, state_half, preferred_element_type=jnp.float32)
    write_total = write_local + jnp.sum(tail_decay[:, :, None] * write_carry, axis=0)
    read_total = read_local + jnp.sum(lead_decay[:, :, None] * read_carry, axis=0)
    grad_write, grad_read = (
        lax.psum_scatter(write_total, "head", scatter_dimension=0, tiled=True),
        lax.psum_scatter(read_total, "head", scatter_dimension=0, tiled=True),
    )
    tok_count = queries.shape[0]
    kv_local = att_keys.shape[1] // HEAD_DIM
    queries4 = queries.reshape(tok_count, kv_local, -1, HEAD_DIM)
    grads4 = out_grad.reshape(tok_count, kv_local, -1, HEAD_DIM)
    scale_factor = HEAD_DIM ** (-0.5)
    own_pair = jnp.stack(
        (
            att_keys.reshape(tok_count, kv_local, HEAD_DIM),
            att_values.reshape(tok_count, kv_local, HEAD_DIM),
        )
    )
    pairs = [own_pair]
    for offset in range(1, REACH + 1):
        pairs.append(shifted(own_pair, "seq", offset))
    key_masks = []
    reaches = []
    for offset in range(REACH + 1):
        block_first = (seq_index - offset) * tok_count
        key_pos = block_first + jnp.arange(tok_count, dtype=jnp.int32)
        key_masks.append(
            (key_pos[None, :] >= first_pos[:, None])
            & (key_pos[None, :] <= element_indices[:, None])
        )
        reaches.append(first_pos[0] <= block_first + tok_count - 1)
    score_list = [
        block_scores(queries4, pairs[offset][0], key_masks[offset], scale_factor)
        for offset in range(REACH + 1)
    ]
    row_max = reduce(jnp.maximum, [jnp.max(item, axis=-1) for item in score_list])
    weight_list = [
        block_weights(score_list[offset], key_masks[offset], row_max) for offset in range(REACH + 1)
    ]
    row_total = reduce(jnp.add, [jnp.sum(item, axis=-1) for item in weight_list])
    probs_list = [item / row_total[..., None] for item in weight_list]
    halves = [item.astype(jnp.bfloat16) for item in probs_list]
    attended = reduce(
        jnp.add, [block_mix(halves[offset], pairs[offset][1]) for offset in range(REACH + 1)]
    )
    delta_rows = jnp.sum(grads4 * attended, axis=-1)
    delta_cols = jnp.transpose(delta_rows, (1, 2, 0))
    query_terms = []
    key_parts = []
    for offset in range(REACH + 1):
        grad_q, pair_part = block_grads(
            queries4,
            grads4,
            pairs[offset][0],
            pairs[offset][1],
            probs_list[offset],
            halves[offset],
            delta_cols,
            scale_factor,
        )
        query_terms.append(grad_q)
        key_parts.append(pair_part)
    grad_query = (
        (reduce(jnp.add, query_terms) * scale_factor).astype(jnp.bfloat16).reshape(tok_count, -1)
    )
    returned = [shifted(key_parts[offset], "seq", -offset) for offset in range(1, REACH + 1)]
    pair_total = key_parts[0] + reduce(jnp.add, returned)
    grad_key = pair_total[0].astype(jnp.bfloat16).reshape(tok_count, -1)
    grad_value = pair_total[1].astype(jnp.bfloat16).reshape(tok_count, -1)
    return (grad_input, grad_write, grad_read, grad_query, grad_key, grad_value)


def solution(mesh):
    placed = (
        P("seq", "head"),
        P("seq", "head"),
        P("seq", None),
        P("seq", None),
        P("head", "seq"),
        P("head"),
        P("head"),
        P("seq", "head"),
        P("seq", "head"),
        P("seq", "head"),
        P("seq", "head"),
        P(),
    )
    return jax.shard_map(
        on_device,
        mesh=mesh,
        in_specs=placed,
        out_specs=(
            P("seq", "head"),
            P(("seq", "head"), None),
            P(("seq", "head"), None),
            P("seq", "head"),
            P("seq", "head"),
            P("seq", "head"),
        ),
        check_vma=False,
    )
```

profile of v0, /device:TPU:120, one launch (start us, length us, event | category | flops | bytes accessed | tf_op | source)
XLA Modules:
  0.0 420.4 jit_solution(3226456512133518119)
XLA Ops:
  19.6 5.0 %collective-permute-start.3 = (bf16[2,256,1,128]{3,1,2,0:T(8,128)(2,1)}, bf16[2,256,1,128]{3,1,2,0:T(8,128)(2,1)}, u32[]{:S(2)}, u32[]{:S(2)}) collective-permute-start(bf16[2,256,1,128]{3,1,2,0:T(8,128)(2,1)} %pad_maximum_fusion.4), channel_id=1, source_target_pairs={{0,32},{8,40},{16,48},{24,56},{32,64},{40,72},{48,80},{56,88},{64,... | collective-permute-start | bytes 393224 | tf_op jit(solution)/shard_map/ppermute | solution.py:35
  24.7 3.1 collective-permute-start.2
  27.8 3.3 collective-permute-start.1
  31.1 4.1 collective-permute-start
  41.9 70.2 %all-reduce = f32[256]{0:T(256)S(1)} all-reduce(f32[256]{0:T(256)S(1)} %dynamic-update-slice), channel_id=2, replica_groups=mesh['seq'=32,'head'=8] {'seq'}, use_global_device_ids=true, to_apply=%add | all-reduce | flops 256 | bytes 2048
  114.3 2.4 convert_reduce_fusion
  116.7 1.8 fusion.4
  127.9 1.3 fusion.80
  129.2 1.3 fusion.48
  133.2 1.9 collective-permute-start.5
  137.8 2.1 collective-permute-start.4
  142.5 1.9 collective-permute-start.6
  147.1 2.0 collective-permute-start.7
  153.2 1.9 fusion.47
  155.0 1.8 copy.323
  156.8 1.3 fusion.50
  158.2 1.3 convolution_bitcast_fusion.17
  159.5 5.6 %collective-permute-done.4 = f32[2,256,1,128]{3,1,2,0:T(8,128)} collective-permute-done((f32[2,256,1,128]{3,1,2,0:T(8,128)}, f32[2,256,1,128]{3,1,2,0:T(8,128)}, u32[]{:S(2)}, u32[]{:S(2)}) %collective-permute-start.4) | collective-permute-done | bytes 262176 | tf_op jit(solution)/shard_map/ppermute | solution.py:35
  168.2 2.9 all-gather.6.cloned.1.call-done
  171.1 11.6 %rev.7 = f32[32,8,128,128]{3,2,1,0:T(8,128)} reverse(f32[32,8,128,128]{3,2,1,0:T(8,128)} %bitcast.557), dimensions={0} | reverse | bytes 33554432 | tf_op jit(solution)/shard_map/rev | solution.py:19
  182.7 58.6 %while.28 = (s32[]{:T(128)}, f32[8,128,128]{2,1,0:T(8,128)S(1)}, s32[]{:T(128)}, f32[32,8]{1,0:T(8,128)}, f32[32,8,128,128]{3,2,1,0:T(8,128)}, /*index=5*/s32[]{:T(128)}, s32[]{:T(128)}) while((s32[]{:T(128)}, f32[8,128,128]{2,1,0:T(8,128)S(1)}, s32[]{:T(128)}, f32[32,8]{1,0:T(8,128)}, f32[32,8,128,128]{3,2,1,0:T(8,128)}, ...), condition=%wide.region_5.6_spmd.clone, body=%wide.region_4.5_spmd.clone.sunk | while | flops 524292 | bytes 1573065 | solution.py:29
  242.7 79.0 %all-gather.8.cloned.1.call-done = f32[256,128,128]{2,1,0:T(8,128)} async-done(((f32[8,128,128]{2,1,0:T(8,128)}), f32[256,128,128]{2,1,0:T(8,128)}) %all-gather.8.cloned.1.call-update) | async-done | bytes 16777232 | tf_op jit(solution)/shard_map/all_gather | solution.py:17
  321.7 58.4 %while.29 = (s32[]{:T(128)}, f32[8,128,128]{2,1,0:T(8,128)S(1)}, s32[]{:T(128)}, f32[32,8]{1,0:T(8,128)}, f32[32,8,128,128]{3,2,1,0:T(8,128)}, /*index=5*/s32[]{:T(128)}, s32[]{:T(128)}) while((s32[]{:T(128)}, f32[8,128,128]{2,1,0:T(8,128)S(1)}, s32[]{:T(128)}, f32[32,8]{1,0:T(8,128)}, f32[32,8,128,128]{3,2,1,0:T(8,128)}, ...), condition=%wide.region_10.11_spmd.clone, body=%wide.region_9.10_spmd.clone.sunk | while | flops 524292 | bytes 1573065 | solution.py:29
  382.7 31.2 %reduce-scatter.5.cloned.1.call-done = f32[32,128]{1,0:T(8,128)} async-done(((f32[256,128]{1,0:T(8,128)}), f32[32,128]{1,0:T(8,128)}) %reduce-scatter.5.cloned.1.call-update) | async-done | bytes 16400 | tf_op jit(solution)/shard_map/reduce_scatter | solution.py:169
  (292 shorter events, 167.0 us)
Async XLA Ops:
  7.2 163.9 %all-gather.6.cloned.1.call-start = ((), (), s32[]{:S(2)}) async-start(), calls=%async_computation.4 | async-start | bytes 17301504 | tf_op jit(solution)/shard_map/all_gather | solution.py:17
  16.1 23.4 %copy-start.15 = (bf16[256,512]{1,0:T(8,128)(2,1)S(1)}, bf16[256,512]{1,0:T(8,128)(2,1)}, u32[]{:S(2)}) copy-start(bf16[256,512]{1,0:T(8,128)(2,1)} %param.26) | copy-start | bytes 786436
  16.1 24.3 %copy-start.33 = (u32[256]{0:T(256)S(1)}, u32[256]{0:T(256)}, u32[]{:S(2)}) copy-start(u32[256]{0:T(256)} %constant.91) | copy-start | bytes 3076
  16.1 305.6 %all-gather.8.cloned.1.call-start = ((), (), s32[]{:S(2)}) async-start(), calls=%async_computation.5 | async-start | bytes 17301504 | tf_op jit(solution)/shard_map/all_gather | solution.py:17
  16.8 96.1 %copy-start.11 = (bf16[256,128]{1,0:T(8,128)(2,1)S(1)}, bf16[256,128]{1,0:T(8,128)(2,1)}, u32[]{:S(2)}) copy-start(bf16[256,128]{1,0:T(8,128)(2,1)} %param.19) | copy-start | bytes 196612
  17.7 21.6 %copy-start.28 = (f32[8]{0:T(128)}, f32[8]{0:T(128)S(1)}, u32[]{:S(2)}) copy-start(f32[8]{0:T(128)S(1)} %get-tuple-element.263) | copy-start | bytes 100
  17.8 21.5 %copy-start.21 = (f32[8,256]{1,0:T(8,128)}, f32[8,256]{1,0:T(8,128)S(1)}, u32[]{:S(2)}) copy-start(f32[8,256]{1,0:T(8,128)S(1)} %exponential_select_fusion.6) | copy-start | bytes 24580
  17.8 95.3 %copy-start.1 = (bf16[256,512]{1,0:T(8,128)(2,1)S(1)}, bf16[256,512]{1,0:T(8,128)(2,1)}, u32[]{:S(2)}) copy-start(bf16[256,512]{1,0:T(8,128)(2,1)} %param.23) | copy-start | bytes 786436
  18.9 363.8 %reduce-scatter.3.cloned.1.call-start = ((), (), s32[]{:S(2)}) async-start(), calls=%async_computation.2 | async-start | bytes 147456 | tf_op jit(solution)/shard_map/reduce_scatter | solution.py:168
  19.6 99.5 %collective-permute-start.3 = (bf16[2,256,1,128]{3,1,2,0:T(8,128)(2,1)}, bf16[2,256,1,128]{3,1,2,0:T(8,128)(2,1)}, u32[]{:S(2)}, u32[]{:S(2)}) collective-permute-start(bf16[2,256,1,128]{3,1,2,0:T(8,128)(2,1)} %pad_maximum_fusion.4), channel_id=1, source_target_pairs={{0,32},{8,40},{16,48},{24,56},{32,64},{40,72},{48,80},{56,88},{64,... | collective-permute-start | bytes 393224 | tf_op jit(solution)/shard_map/ppermute | solution.py:35
  24.7 95.6 %collective-permute-start.2 = (bf16[2,256,1,128]{3,1,2,0:T(8,128)(2,1)}, bf16[2,256,1,128]{3,1,2,0:T(8,128)(2,1)}, u32[]{:S(2)}, u32[]{:S(2)}) collective-permute-start(bf16[2,256,1,128]{3,1,2,0:T(8,128)(2,1)} %pad_maximum_fusion.4), channel_id=1, source_target_pairs={{0,24},{8,32},{16,40},{24,48},{32,56},{40,64},{48,72},{56,80},{64,... | collective-permute-start | bytes 393224 | tf_op jit(solution)/shard_map/ppermute | solution.py:35
  27.8 93.7 %collective-permute-start.1 = (bf16[2,256,1,128]{3,1,2,0:T(8,128)(2,1)}, bf16[2,256,1,128]{3,1,2,0:T(8,128)(2,1)}, u32[]{:S(2)}, u32[]{:S(2)}) collective-permute-start(bf16[2,256,1,128]{3,1,2,0:T(8,128)(2,1)} %pad_maximum_fusion.4), channel_id=1, source_target_pairs={{0,16},{8,24},{16,32},{24,40},{32,48},{40,56},{48,64},{56,72},{64,... | collective-permute-start | bytes 393224 | tf_op jit(solution)/shard_map/ppermute | solution.py:35
  31.1 91.6 %collective-permute-start = (bf16[2,256,1,128]{3,1,2,0:T(8,128)(2,1)}, bf16[2,256,1,128]{3,1,2,0:T(8,128)(2,1)}, u32[]{:S(2)}, u32[]{:S(2)}) collective-permute-start(bf16[2,256,1,128]{3,1,2,0:T(8,128)(2,1)} %pad_maximum_fusion.4), channel_id=1, source_target_pairs={{0,8},{8,16},{16,24},{24,32},{32,40},{40,48},{48,56},{56,64},{64,7... | collective-permute-start | bytes 393224 | tf_op jit(solution)/shard_map/ppermute | solution.py:35
  123.9 25.2 %copy-start.24 = (f32[4,256]{1,0:T(4,128)}, f32[4,256]{1,0:T(4,128)S(1)}, u32[]{:S(2)}) copy-start(f32[4,256]{1,0:T(4,128)S(1)} %maximum_maximum_fusion) | copy-start | bytes 12292
  124.9 24.2 %copy-start.30 = (f32[4,256]{1,0:T(4,128)}, f32[4,256]{1,0:T(4,128)S(1)}, u32[]{:S(2)}) copy-start(f32[4,256]{1,0:T(4,128)S(1)} %add_add_fusion) | copy-start | bytes 12292
  133.2 26.3 %collective-permute-start.5 = (f32[2,256,1,128]{3,1,2,0:T(8,128)}, f32[2,256,1,128]{3,1,2,0:T(8,128)}, u32[]{:S(2)}, u32[]{:S(2)}) collective-permute-start(f32[2,256,1,128]{3,1,2,0:T(8,128)} %pad_maximum_fusion.1), channel_id=1, source_target_pairs={{16,0},{24,8},{32,16},{40,24},{48,32},{56,40},{64,48},{72,56},{80,... | collective-permute-start | bytes 786440 | tf_op jit(solution)/shard_map/ppermute | solution.py:35
  137.8 27.3 %collective-permute-start.4 = (f32[2,256,1,128]{3,1,2,0:T(8,128)}, f32[2,256,1,128]{3,1,2,0:T(8,128)}, u32[]{:S(2)}, u32[]{:S(2)}) collective-permute-start(f32[2,256,1,128]{3,1,2,0:T(8,128)} %pad_maximum_fusion), channel_id=1, source_target_pairs={{8,0},{16,8},{24,16},{32,24},{40,32},{48,40},{56,48},{64,56},{72,6... | collective-permute-start | bytes 786440 | tf_op jit(solution)/shard_map/ppermute | solution.py:35
  142.5 22.6 %collective-permute-start.6 = (f32[2,256,1,128]{3,1,2,0:T(8,128)}, f32[2,256,1,128]{3,1,2,0:T(8,128)}, u32[]{:S(2)}, u32[]{:S(2)}) collective-permute-start(f32[2,256,1,128]{3,1,2,0:T(8,128)} %pad_maximum_fusion.2), channel_id=1, source_target_pairs={{24,0},{32,8},{40,16},{48,24},{56,32},{64,40},{72,48},{80,56},{88,... | collective-permute-start | bytes 786440 | tf_op jit(solution)/shard_map/ppermute | solution.py:35
  147.1 19.2 %collective-permute-start.7 = (f32[2,256,1,128]{3,1,2,0:T(8,128)}, f32[2,256,1,128]{3,1,2,0:T(8,128)}, u32[]{:S(2)}, u32[]{:S(2)}) collective-permute-start(f32[2,256,1,128]{3,1,2,0:T(8,128)} %pad_maximum_fusion.3), channel_id=1, source_target_pairs={{32,0},{40,8},{48,16},{56,24},{64,32},{72,40},{80,48},{88,56},{96,... | collective-permute-start | bytes 786440 | tf_op jit(solution)/shard_map/ppermute | solution.py:35
  182.7 58.6 %copy-start.22 = (f32[8,256]{1,0:T(8,128)S(1)}, f32[8,256]{1,0:T(8,128)}, u32[]{:S(2)}) copy-start(f32[8,256]{1,0:T(8,128)} %copy-done.21) | copy-start | bytes 24580
  182.7 59.0 %copy-start.12 = (bf16[256,128]{1,0:T(8,128)(2,1)S(1)}, bf16[256,128]{1,0:T(8,128)(2,1)}, u32[]{:S(2)}) copy-start(bf16[256,128]{1,0:T(8,128)(2,1)} %param.19) | copy-start | bytes 196612
  182.7 59.0 %copy-start.13 = (bf16[256,256]{1,0:T(8,128)(2,1)S(1)}, bf16[256,256]{1,0:T(8,128)(2,1)}, u32[]{:S(2)}) copy-start(bf16[256,256]{1,0:T(8,128)(2,1)} %convert_reduce_fusion) | copy-start | bytes 393220
  242.6 171.2 %reduce-scatter.5.cloned.1.call-start = ((), (), s32[]{:S(2)}) async-start(), calls=%async_computation.3 | async-start | bytes 147456 | tf_op jit(solution)/shard_map/reduce_scatter | solution.py:169
  321.7 59.6 %copy-start.23 = (f32[256,8]{0,1:T(8,128)S(1)}, f32[256,8]{0,1:T(8,128)}, u32[]{:S(2)}) copy-start(f32[256,8]{0,1:T(8,128)} %fusion.199) | copy-start | bytes 24580
  (22 other events, 81.6 us)
Sparse Core Ops, SparseCore 0:
  16.2 154.8 all-gather.5
  173.7 147.9 all-gather.7
  324.8 32.2 reduce-scatter.2
  381.4 32.3 reduce-scatter.4
where the time goes:
time: 428 us; the launch traced here: 420 us
  waiting for transfers between devices  120 us (28%)
  other arithmetic  84.9 us (20%)
  blocking collectives  70.2 us (16%)
  local copies, waits for them, and re-layouts  68.8 us (16%)
  matrix products  36.5 us (9%)
  starting transfers between devices  23.6 us (6%)
  between operations  15.2 us (4%)
    all_gather x2, waiting for transfers between devices, carried_in(): pieces = jax.tree.map(lambda part: lax.all_gather(part, axis), value)  81.9 us
    select_n x62, other arithmetic, lap(): jnp.where(position < mine, new, old)  72.6 us
    unnamed x1, blocking collectives  70.2 us
    mul x62, local copies, waits for them, and re-layouts, chain_combine(): latter[0][:, None, None] * earlier[1] + latter[1]  43.2 us
    reduce_scatter x1, waiting for transfers between devices, on_device(): lax.psum_scatter(read_total, 'head', scatter_dimension=0, tiled=True)  31.2 us
    ppermute x8, starting transfers between devices, shifted(): return lax.ppermute(block, axis, route)  23.5 us
    rev x2, local copies, waits for them, and re-layouts, carried_in(): pieces = jax.tree.map(lambda part: part[::-1], pieces)  12.2 us
  transfers between devices with their start and end apart: 12, of which 5 were waited for; matrix products, arithmetic and copies ran while one was open for 43% of the time, Pallas kernels for 0%

commit v1 on v0

v1 whole, which is shorter than its diff:
```python
import functools
import math

import jax
import jax.numpy as jnp
from jax import lax
from jax.experimental import pallas as pl
from jax.experimental.pallas import tpu as pltpu
from jax.sharding import PartitionSpec as P

MESH = pl.DeviceIdType.MESH
REACH = 4
DIM = 128
NEG = -1e30
SCALE = DIM ** (-0.5)
SCALE2 = SCALE * math.log2(math.e)
SHIFT = 1

F32 = jnp.float32
BF16 = jnp.bfloat16


def nn(a, b):
    return jnp.dot(a, b, preferred_element_type=F32)


def nt(a, b):
    return lax.dot_general(a, b, (((1,), (1,)), ((), ())), preferred_element_type=F32)


def flip(a):
    return jnp.transpose(a.astype(F32))


def cols(h):
    return pl.ds(pl.multiple_of(h * DIM, DIM), DIM)


def kernel(
    n_seq,
    n_head,
    x_ref,
    g_ref,
    w_ref,
    r_ref,
    step_ref,
    rate_ref,
    gain_ref,
    q_ref,
    k_ref,
    v_ref,
    og_ref,
    doc_ref,
    gi_ref,
    gw_ref,
    gr_ref,
    gq_ref,
    gk_ref,
    gv_ref,
    kv,
    kt,
    dacc,
    dkv_out,
    dkv_in,
    cbuf,
    st_out,
    st_in,
    wt,
    rt,
    rows,
    run_col,
    tail_col,
    lead_col,
    gi_acc,
    w_acc,
    coef,
    tot,
    rs_in,
    kv_send,
    kv_recv,
    c_send,
    c_recv,
    st_send,
    st_recv,
    dkv_send,
    dkv_recv,
    rs_send,
    rs_recv,
):
    tok = x_ref.shape[0]
    heads = step_ref.shape[0]
    q_heads = q_ref.shape[1] // DIM
    me = lax.axis_index("seq")
    hd = lax.axis_index("head")

    def seq_at(d):
        return lax.rem(me + (d + n_seq), n_seq)

    def head_at(p):
        return lax.rem(hd + p, n_head)

    def push(src, dst, send, recv, to):
        return pltpu.make_async_remote_copy(
            src_ref=src, dst_ref=dst, send_sem=send, recv_sem=recv, device_id=to, device_id_type=MESH
        )

    barrier = pltpu.get_barrier_semaphore()
    offsets = [d for d in range(-REACH, REACH + 1) if d]
    for d in offsets:
        pl.semaphore_signal(barrier, inc=1, device_id=(seq_at(d), hd), device_id_type=MESH)
    for p in range(1, n_head):
        pl.semaphore_signal(barrier, inc=1, device_id=(me, head_at(p)), device_id_type=MESH)

    kv[0, 0] = k_ref[...]
    kv[0, 1] = v_ref[...]

    pl.semaphore_wait(barrier, len(offsets) + n_head - 1)

    kv_copies = {}
    for d in (4, 1, 3, 2):
        kv_copies[d] = push(
            kv.at[0], kv.at[d], kv_send.at[d - 1], kv_recv.at[d - 1], (seq_at(d), hd)
        )
        kv_copies[d].start()

    base = (me * tok).astype(F32)
    lens = jnp.broadcast_to(doc_ref[...].astype(F32), (DIM, DIM))
    i0 = lax.broadcasted_iota(jnp.int32, (DIM, DIM), 0)
    i1 = lax.broadcasted_iota(jnp.int32, (DIM, DIM), 1)
    first_c = jnp.sum(jnp.where(i1 < i0, lens, 0.0), axis=1, keepdims=True)
    lens_c = jnp.sum(jnp.where(i1 == i0, lens, 0.0), axis=1, keepdims=True)
    first_r = jnp.sum(jnp.where(i0 < i1, lens_c, 0.0), axis=0, keepdims=True)
    t_row = base + lax.broadcasted_iota(jnp.int32, (1, tok), 1).astype(F32)
    t_col = base + lax.broadcasted_iota(jnp.int32, (tok, 1), 0).astype(F32)
    fp_row = jnp.max(jnp.where(first_c <= t_row, first_c, 0.0), axis=0, keepdims=True)
    fp_col = jnp.max(jnp.where(first_r <= t_col, first_r, 0.0), axis=1, keepdims=True)
    fp_last = fp_row[:, tok - 1 : tok]

    sub = lax.broadcasted_iota(jnp.int32, (heads, 1), 0)
    rate = jnp.zeros((heads, 1), F32)
    for h in range(heads):
        rate = jnp.where(sub == h, rate_ref[h], rate)
    decay = -(rate * step_ref[...])
    j0 = lax.broadcasted_iota(jnp.int32, (tok, tok), 0)
    j1 = lax.broadcasted_iota(jnp.int32, (tok, tok), 1)
    run_r = jnp.dot(
        decay,
        (j0 <= j1).astype(F32),
        preferred_element_type=F32,
        precision=lax.Precision.HIGHEST,
    )
    run_c = lax.dot_general(
        (j1 <= j0).astype(F32),
        decay,
        (((1,), (1,)), ((), ())),
        preferred_element_type=F32,
        precision=lax.Precision.HIGHEST,
    )
    total_c = run_r[:, tok - 1 : tok]
    total_r = run_c[tok - 1 : tok, :]
    rows[0] = run_r
    rows[1] = jnp.where(fp_row == fp_last, jnp.exp(total_c - run_r), 0.0)
    rows[2] = jnp.where(fp_row < base, jnp.exp(run_r), 0.0)
    cbuf[3] = jnp.broadcast_to(jnp.where(fp_last < base, jnp.exp(total_c), 0.0), (heads, DIM))
    c_copies = []
    for i, d in enumerate((-3, -2, -1, 1, 2, 3)):
        copy = push(cbuf.at[3], cbuf.at[3 - d], c_send.at[i], c_recv.at[3 - d], (seq_at(d), hd))
        copy.start()
        c_copies.append(copy)

    wt[...] = flip(w_ref[...])
    rt[...] = flip(r_ref[...])

    def part_loop(h, _):
        scaled_w = (wt[...] * rows[1, pl.ds(h, 1), :]).astype(BF16)
        scaled_r = (rt[...] * rows[2, pl.ds(h, 1), :]).astype(BF16)
        st_out[0, 0, h] = nn(scaled_w, x_ref[:, cols(h)]).astype(BF16)
        st_out[1, 0, h] = nn(scaled_r, g_ref[:, cols(h)]).astype(BF16)
        return 0

    lax.fori_loop(0, heads, part_loop, 0)

    pos = (lax.rem(me, 4), lax.rem(3 + SHIFT + n_seq - me, 4))
    sign = (1, -1)
    st_copies = {}

    def send_state(which, stage):
        y = pos[which]
        if stage == 0:
            step = 1 - 2 * lax.rem(y, 2)
        elif stage == 1:
            step = 3 - 2 * y
        else:
            step = 4
        to = lax.rem(me + sign[which] * step + n_seq, n_seq)
        copy = push(
            st_out.at[which, stage],
            st_in.at[which, stage],
            st_send.at[which, stage],
            st_recv.at[which, stage],
            (to, hd),
        )
        copy.start()
        st_copies[which, stage] = copy

    send_state(0, 0)
    send_state(1, 0)

    tail_c = jnp.where(fp_col == fp_last, jnp.exp(total_r - run_c), 0.0)
    lead_c = jnp.where(fp_col < base, jnp.exp(run_c), 0.0)
    for h in range(heads):
        run_col[h] = run_c[:, h : h + 1]
        tail_col[h] = tail_c[:, h : h + 1]
        lead_col[h] = lead_c[:, h : h + 1]

    cross = nt(w_ref[...], r_ref[...])
    keep = (j0 <= j1) & (fp_col == fp_row)
    w_acc[...] = jnp.zeros_like(w_acc)

    def local_loop(h, _):
        x_h = x_ref[:, cols(h)]
        g_h = g_ref[:, cols(h)]
        corr = nt(x_h, g_h)
        dec = jnp.exp(jnp.where(keep, rows[0, pl.ds(h, 1), :] - run_col[h], NEG))
        w_acc[...] += corr * dec
        mix = (cross * dec).astype(BF16)
        gi_acc[:, cols(h)] = nn(mix, g_h) + gain_ref[h] * g_h.astype(F32)
        return 0

    lax.fori_loop(0, heads, local_loop, 0)
    w_sum = w_acc[...]
    gw = nn(w_sum.astype(BF16), r_ref[...])
    gr = nn(flip(w_sum).astype(BF16), w_ref[...])
    for c in range(n_head):
        tot[c, 0] = gw[c * (tok // n_head) : (c + 1) * (tok // n_head)]
        tot[c, 1] = gr[c * (tok // n_head) : (c + 1) * (tok // n_head)]

    for copy in c_copies:
        copy.wait_recv()
    for which in (0, 1):
        y, s = pos[which], sign[which]
        c0, c1, c2, c3 = [cbuf[3 + s * (q - y)] for q in range(4)]
        own, after = cbuf[3], cbuf[3 + s]
        odd = lax.rem(y, 2) == 1
        one, zero = jnp.ones_like(own), jnp.zeros_like(own)
        coef[which, 0] = jnp.where(odd, one, after)
        coef[which, 1] = jnp.where(odd, own, one)
        coef[which, 2] = jnp.where(y < 2, c2 * c3, one)
        coef[which, 3] = jnp.where(y < 2, one, zero)
        coef[which, 4] = jnp.where(odd, one, zero)
        coef[which, 5] = jnp.where(y == 2, one, jnp.where(y == 3, c2, zero))
        coef[which, 6] = jnp.where(
            y == 0, one, jnp.where(y == 1, c0, jnp.where(y == 2, c0 * c1, c0 * c1 * c2))
        )

    def factor(which, i, h):
        return coef[which, i, pl.ds(h, 1), :]

    for which in (0, 1):
        st_copies[which, 0].wait_recv()

        def pair_loop(h, _, which=which):
            st_out[which, 1, h] = (
                factor(which, 0, h) * st_out[which, 0, h].astype(F32)
                + factor(which, 1, h) * st_in[which, 0, h].astype(F32)
            ).astype(BF16)
            return 0

        lax.fori_loop(0, heads, pair_loop, 0)
        send_state(which, 1)

    for d in (4, 1, 3, 2):
        kv_copies[d].wait_recv()
    for o in range(REACH + 1):
        kt[o] = flip(kv[o, 0]).astype(BF16)
    dacc[...] = jnp.zeros_like(dacc)
    spot = lax.broadcasted_iota(jnp.int32, (tok, 1), 0).astype(F32)

    def attend(i, _):
        q_i = q_ref[:, cols(i)]
        og_i = og_ref[:, cols(i)]
        scores = []
        for o in range(REACH + 1):
            key_pos = spot + (base - float(o * tok))
            allowed = key_pos >= fp_row
            if o == 0:
                allowed = allowed & (key_pos <= t_row)
            scores.append(jnp.where(allowed, nt(kv[o, 0], q_i) * SCALE2, NEG))
        top = functools.reduce(jnp.maximum, [jnp.max(s, axis=0, keepdims=True) for s in scores])
        weights = [jnp.exp2(s - top) for s in scores]
        norm = 1.0 / functools.reduce(
            jnp.add, [jnp.sum(e, axis=0, keepdims=True) for e in weights]
        )
        probs = [e * norm for e in weights]
        halves = [p.astype(BF16) for p in probs]
        dprob = [nt(kv[o, 1], og_i) for o in range(REACH + 1)]
        delta = functools.reduce(
            jnp.add,
            [
                jnp.sum(halves[o].astype(F32) * dprob[o], axis=0, keepdims=True)
                for o in range(REACH + 1)
            ],
        )
        dq = jnp.zeros((DIM, tok), F32)
        for o in range(REACH + 1):
            ds = (probs[o] * (dprob[o] - delta)).astype(BF16)
            dacc[o, 0] += nn(ds, q_i)
            dacc[o, 1] += nn(halves[o], og_i)
            dq += nn(kt[o], ds)
        gq_ref[:, cols(i)] = (jnp.transpose(dq) * SCALE).astype(BF16)
        return 0

    lax.fori_loop(0, q_heads // 2, attend, 0)

    for which in (0, 1):
        st_copies[which, 1].wait_recv()
        base_at = 1 - lax.rem(pos[which], 2)

        def reach_loop(h, _, which=which, base_at=base_at):
            st_out[which, 2, h] = (
                factor(which, 2, h) * st_out[which, base_at, h].astype(F32)
                + factor(which, 3, h) * st_in[which, 1, h].astype(F32)
            ).astype(BF16)
            return 0

        lax.fori_loop(0, heads, reach_loop, 0)
        send_state(which, 2)

    lax.fori_loop(q_heads // 2, q_heads, attend, 0)

    dkv_copies = {}
    for d in (4, 2, 3, 1):
        dkv_out[d - 1, 0] = (dacc[d, 0] * SCALE).astype(BF16)
        dkv_out[d - 1, 1] = dacc[d, 1].astype(BF16)
        dkv_copies[d] = push(
            dkv_out.at[d - 1],
            dkv_in.at[d - 1],
            dkv_send.at[d - 1],
            dkv_recv.at[d - 1],
            (seq_at(-d), hd),
        )
        dkv_copies[d].start()

    for which in (0, 1):
        st_copies[which, 2].wait_recv()

    def arrived(which, h):
        return (
            factor(which, 4, h) * st_in[which, 0, h].astype(F32)
            + factor(which, 5, h) * st_in[which, 1, h].astype(F32)
            + factor(which, 6, h) * st_in[which, 2, h].astype(F32)
        ).astype(BF16)

    def carry_loop(h, sums):
        state, adjoint = arrived(0, h), arrived(1, h)
        x_h = x_ref[:, cols(h)]
        g_h = g_ref[:, cols(h)]
        tail_h, lead_h = tail_col[h], lead_col[h]
        gi_ref[:, cols(h)] = (gi_acc[:, cols(h)] + nn(w_ref[...], adjoint) * tail_h).astype(BF16)
        return (
            sums[0] + nt(x_h, adjoint) * tail_h,
            sums[1] + nt(g_h, state) * lead_h,
        )

    zeros = jnp.zeros((tok, DIM), F32)
    gw, gr = lax.fori_loop(0, heads, carry_loop, (zeros, zeros))
    rows_each = tok // n_head
    for c in range(n_head):
        tot[c, 0] += gw[c * rows_each : (c + 1) * rows_each]
        tot[c, 1] += gr[c * rows_each : (c + 1) * rows_each]
    rs_copies = []
    for p in range(1, n_head):
        to = head_at(p)
        copy = push(tot.at[to], rs_in.at[p - 1], rs_send.at[p - 1], rs_recv.at[p - 1], (me, to))
        copy.start()
        rs_copies.append(copy)

    gk = dacc[0, 0] * SCALE
    gv = dacc[0, 1]
    for d in (4, 2, 3, 1):
        dkv_copies[d].wait_recv()
        gk += dkv_in[d - 1, 0].astype(F32)
        gv += dkv_in[d - 1, 1].astype(F32)
    gk_ref[...] = gk.astype(BF16)
    gv_ref[...] = gv.astype(BF16)

    gw_out = tot[hd, 0]
    gr_out = tot[hd, 1]
    for p in range(1, n_head):
        rs_copies[p - 1].wait_recv()
        gw_out += rs_in[p - 1, 0]
        gr_out += rs_in[p - 1, 1]
    gw_ref[...] = gw_out
    gr_ref[...] = gr_out

    for copy in kv_copies.values():
        copy.wait_send()
    for copy in c_copies:
        copy.wait_send()
    for copy in st_copies.values():
        copy.wait_send()
    for copy in dkv_copies.values():
        copy.wait_send()
    for copy in rs_copies:
        copy.wait_send()


def on_device(n_seq, n_head, *args):
    (x, g, w, r, step, rate, gain, q, k, v, og, docs) = args
    tok, heads = x.shape[0], step.shape[0]
    vmem = pl.BlockSpec(memory_space=pltpu.VMEM)
    smem = pl.BlockSpec(memory_space=pltpu.SMEM)
    rows_each = tok // n_head
    dma = pltpu.SemaphoreType.DMA
    scratch = [
        pltpu.VMEM((REACH + 1, 2, tok, DIM), BF16),
        pltpu.VMEM((REACH + 1, DIM, tok), BF16),
        pltpu.VMEM((REACH + 1, 2, tok, DIM), F32),
        pltpu.VMEM((REACH, 2, tok, DIM), BF16),
        pltpu.VMEM((REACH, 2, tok, DIM), BF16),
        pltpu.VMEM((7, heads, DIM), F32),
        pltpu.VMEM((2, 3, heads, DIM, DIM), BF16),
        pltpu.VMEM((2, 3, heads, DIM, DIM), BF16),
        pltpu.VMEM((DIM, tok), F32),
        pltpu.VMEM((DIM, tok), F32),
        pltpu.VMEM((3, heads, tok), F32),
        pltpu.VMEM((heads, tok, 1), F32),
        pltpu.VMEM((heads, tok, 1), F32),
        pltpu.VMEM((heads, tok, 1), F32),
        pltpu.VMEM((tok, heads * DIM), F32),
        pltpu.VMEM((tok, tok), F32),
        pltpu.VMEM((2, 7, heads, DIM), F32),
        pltpu.VMEM((n_head, 2, rows_each, DIM), F32),
        pltpu.VMEM((n_head - 1, 2, rows_each, DIM), F32),
        dma((REACH,)),
        dma((REACH,)),
        dma((6,)),
        dma((7,)),
        dma((2, 3)),
        dma((2, 3)),
        dma((REACH,)),
        dma((REACH,)),
        dma((n_head - 1,)),
        dma((n_head - 1,)),
    ]
    return pl.pallas_call(
        functools.partial(kernel, n_seq, n_head),
        out_shape=(
            jax.ShapeDtypeStruct(x.shape, BF16),
            jax.ShapeDtypeStruct((rows_each, DIM), F32),
            jax.ShapeDtypeStruct((rows_each, DIM), F32),
            jax.ShapeDtypeStruct(q.shape, BF16),
            jax.ShapeDtypeStruct(k.shape, BF16),
            jax.ShapeDtypeStruct(v.shape, BF16),
        ),
        in_specs=[vmem] * 5 + [smem] * 2 + [vmem] * 5,
        out_specs=(vmem,) * 6,
        scratch_shapes=scratch,
        compiler_params=pltpu.CompilerParams(
            collective_id=0, has_side_effects=True, vmem_limit_bytes=48 * 2**20
        ),
    )(x, g, w, r, step, rate, gain, q, k, v, og, docs.reshape(1, -1))


def solution(mesh):
    placed = (
        P("seq", "head"),
        P("seq", "head"),
        P("seq", None),
        P("seq", None),
        P("head", "seq"),
        P("head"),
        P("head"),
        P("seq", "head"),
        P("seq", "head"),
        P("seq", "head"),
        P("seq", "head"),
        P(),
    )
    return jax.shard_map(
        functools.partial(on_device, mesh.shape["seq"], mesh.shape["head"]),
        mesh=mesh,
        in_specs=placed,
        out_specs=(
            P("seq", "head"),
            P(("seq", "head"), None),
            P(("seq", "head"), None),
            P("seq", "head"),
            P("seq", "head"),
            P("seq", "head"),
        ),
        check_vma=False,
    )
```

time: 428 us -> 67.6 us (0.16)
  the two profiles are of different devices: /device:TPU:120 before, /device:TPU:1 now
where the time goes in v1:
time: 67.6 us; the launch traced here: 67.1 us
  Pallas kernels  53.8 us (80%)
  local copies, waits for them, and re-layouts  12.7 us (19%)
  between operations  0.68 us (1%)
    pallas_call x1, Pallas kernels, on_device(): pl.pallas_call(functools.partial(kernel, n_seq, n_head), out_shape=(jax.S...  53.8 us
    unnamed x30, local copies, waits for them, and re-layouts  12.7 us

profile of v1, /device:TPU:1, one launch (start us, length us, event | category | flops | bytes accessed | tf_op | source)
XLA Modules:
  0.0 67.1 jit_solution(12404035296802713742)
XLA Ops:
  0.6 0.0 copy-start.11
  0.6 0.0 copy-start.10
  0.7 0.0 copy-start.9
  0.7 0.6 copy-done.11
  1.3 0.0 copy-done.10
  1.3 0.0 copy-done.9
  1.3 0.0 copy-start
  1.3 1.0 %copy-done = bf16[256,1024]{1,0:T(8,128)(2,1)S(1)} copy-done((bf16[256,1024]{1,0:T(8,128)(2,1)S(1)}, bf16[256,1024]{1,0:T(8,128)(2,1)}, u32[]{:S(2)}) %copy-start) | copy-done | bytes 524312
  2.4 0.0 copy-start.1
  2.4 1.0 %copy-done.1 = bf16[256,1024]{1,0:T(8,128)(2,1)S(1)} copy-done((bf16[256,1024]{1,0:T(8,128)(2,1)S(1)}, bf16[256,1024]{1,0:T(8,128)(2,1)}, u32[]{:S(2)}) %copy-start.1) | copy-done | bytes 524312
  3.4 0.9 %copy-done.2 = bf16[256,512]{1,0:T(8,128)(2,1)S(1)} copy-done((bf16[256,512]{1,0:T(8,128)(2,1)S(1)}, bf16[256,512]{1,0:T(8,128)(2,1)}, u32[]{:S(2)}) %copy-start.2) | copy-done | bytes 262168
  4.4 0.9 %copy-done.3 = bf16[256,512]{1,0:T(8,128)(2,1)S(1)} copy-done((bf16[256,512]{1,0:T(8,128)(2,1)S(1)}, bf16[256,512]{1,0:T(8,128)(2,1)}, u32[]{:S(2)}) %copy-start.3) | copy-done | bytes 262168
  5.3 0.8 %copy-done.4 = bf16[256,128]{1,0:T(8,128)(2,1)S(1)} copy-done((bf16[256,128]{1,0:T(8,128)(2,1)S(1)}, bf16[256,128]{1,0:T(8,128)(2,1)}, u32[]{:S(2)}) %copy-start.4) | copy-done | bytes 65560
  6.2 0.8 %copy-done.5 = bf16[256,128]{1,0:T(8,128)(2,1)S(1)} copy-done((bf16[256,128]{1,0:T(8,128)(2,1)S(1)}, bf16[256,128]{1,0:T(8,128)(2,1)}, u32[]{:S(2)}) %copy-start.5) | copy-done | bytes 65560
  7.0 0.8 %copy-done.6 = bf16[256,128]{1,0:T(8,128)(2,1)S(1)} copy-done((bf16[256,128]{1,0:T(8,128)(2,1)S(1)}, bf16[256,128]{1,0:T(8,128)(2,1)}, u32[]{:S(2)}) %copy-start.6) | copy-done | bytes 65560
  7.8 0.8 %copy-done.7 = bf16[256,128]{1,0:T(8,128)(2,1)S(1)} copy-done((bf16[256,128]{1,0:T(8,128)(2,1)S(1)}, bf16[256,128]{1,0:T(8,128)(2,1)}, u32[]{:S(2)}) %copy-start.7) | copy-done | bytes 65560
  8.7 0.7 %copy-done.8 = f32[8,256]{1,0:T(8,128)S(1)} copy-done((f32[8,256]{1,0:T(8,128)S(1)}, f32[8,256]{1,0:T(8,128)}, u32[]{:S(2)}) %copy-start.8) | copy-done | bytes 8216
  9.4 53.8 %shard_map.163 = (bf16[256,1024]{1,0:T(8,128)(2,1)S(1)}, f32[32,128]{1,0:T(8,128)S(1)}, f32[32,128]{1,0:T(8,128)S(1)}, bf16[256,512]{1,0:T(8,128)(2,1)S(1)}, bf1...) custom-call(bf16[256,1024]{1,0:T(8,128)(2,1)S(1)} %copy-done, bf16[256,1024]{1,0:T(8,128)(2,1)S(1)} %copy-done.1, ...), custom_call_target="tpu_custom_call" | custom-call | tf_op jit(solution)/shard_map/pallas_call | solution.py:446
  63.1 0.8 %copy.24 = bf16[256,1024]{1,0:T(8,128)(2,1)} copy(bf16[256,1024]{1,0:T(8,128)(2,1)S(1)} %get-tuple-element.12) | data formatting | bytes 1048576
  63.9 0.6 copy.25
  64.5 0.6 copy.26
  65.1 0.7 %copy.27 = bf16[256,512]{1,0:T(8,128)(2,1)} copy(bf16[256,512]{1,0:T(8,128)(2,1)S(1)} %get-tuple-element.15) | data formatting | bytes 524288
  65.8 0.6 copy.28
  66.5 0.6 copy.29
  (7 shorter events, 0.0 us)
Async XLA Ops:
  0.6 0.7 copy-start.11
  0.6 0.7 copy-start.10
  0.7 0.7 copy-start.9
  1.3 1.0 %copy-start = (bf16[256,1024]{1,0:T(8,128)(2,1)S(1)}, bf16[256,1024]{1,0:T(8,128)(2,1)}, u32[]{:S(2)}) copy-start(bf16[256,1024]{1,0:T(8,128)(2,1)} %x_ref.1) | copy-start | bytes 1572868
  2.4 1.0 %copy-start.1 = (bf16[256,1024]{1,0:T(8,128)(2,1)S(1)}, bf16[256,1024]{1,0:T(8,128)(2,1)}, u32[]{:S(2)}) copy-start(bf16[256,1024]{1,0:T(8,128)(2,1)} %g_ref.1) | copy-start | bytes 1572868
  3.4 0.9 %copy-start.2 = (bf16[256,512]{1,0:T(8,128)(2,1)S(1)}, bf16[256,512]{1,0:T(8,128)(2,1)}, u32[]{:S(2)}) copy-start(bf16[256,512]{1,0:T(8,128)(2,1)} %q_ref.1) | copy-start | bytes 786436
  4.4 0.9 %copy-start.3 = (bf16[256,512]{1,0:T(8,128)(2,1)S(1)}, bf16[256,512]{1,0:T(8,128)(2,1)}, u32[]{:S(2)}) copy-start(bf16[256,512]{1,0:T(8,128)(2,1)} %og_ref.1) | copy-start | bytes 786436
  5.3 0.8 %copy-start.4 = (bf16[256,128]{1,0:T(8,128)(2,1)S(1)}, bf16[256,128]{1,0:T(8,128)(2,1)}, u32[]{:S(2)}) copy-start(bf16[256,128]{1,0:T(8,128)(2,1)} %w_ref.1) | copy-start | bytes 196612
  6.2 0.8 %copy-start.5 = (bf16[256,128]{1,0:T(8,128)(2,1)S(1)}, bf16[256,128]{1,0:T(8,128)(2,1)}, u32[]{:S(2)}) copy-start(bf16[256,128]{1,0:T(8,128)(2,1)} %r_ref.1) | copy-start | bytes 196612
  7.0 0.8 %copy-start.6 = (bf16[256,128]{1,0:T(8,128)(2,1)S(1)}, bf16[256,128]{1,0:T(8,128)(2,1)}, u32[]{:S(2)}) copy-start(bf16[256,128]{1,0:T(8,128)(2,1)} %k_ref.1) | copy-start | bytes 196612
  7.8 0.8 %copy-start.7 = (bf16[256,128]{1,0:T(8,128)(2,1)S(1)}, bf16[256,128]{1,0:T(8,128)(2,1)}, u32[]{:S(2)}) copy-start(bf16[256,128]{1,0:T(8,128)(2,1)} %v_ref.1) | copy-start | bytes 196612
  8.7 0.7 %copy-start.8 = (f32[8,256]{1,0:T(8,128)S(1)}, f32[8,256]{1,0:T(8,128)}, u32[]{:S(2)}) copy-start(f32[8,256]{1,0:T(8,128)} %step_ref.1) | copy-start | bytes 24580

commit v2 on v1

--- a/solution.py
+++ b/solution.py
@@ -15,6 +15,8 @@
 SCALE = DIM ** (-0.5)
 SCALE2 = SCALE * math.log2(math.e)
 SHIFT = 1
+CHUNKS = 4
+KV_ROW = True
 
 F32 = jnp.float32
 BF16 = jnp.bfloat16
@@ -39,6 +41,24 @@
 def kernel(
     n_seq,
     n_head,
+    x_hbm,
+    g_hbm,
+    w_hbm,
+    r_hbm,
+    step_hbm,
+    rate_hbm,
+    gain_hbm,
+    q_hbm,
+    k_hbm,
+    v_hbm,
+    og_hbm,
+    doc_hbm,
+    gi_ref,
+    gw_ref,
+    gr_ref,
+    gq_ref,
+    gk_ref,
+    gv_ref,
     x_ref,
     g_ref,
     w_ref,
@@ -47,19 +67,15 @@
     rate_ref,
     gain_ref,
     q_ref,
-    k_ref,
-    v_ref,
     og_ref,
     doc_ref,
-    gi_ref,
-    gw_ref,
-    gr_ref,
-    gq_ref,
-    gk_ref,
-    gv_ref,
     kv,
     kt,
-    dacc,
+    q_rows,
+    og_rows,
+    ds_all,
+    ph_all,
+    own_grad,
     dkv_out,
     dkv_in,
     cbuf,
@@ -75,7 +91,9 @@
     w_acc,
     coef,
     tot,
+    rs_out,
     rs_in,
+    load_sem,
     kv_send,
     kv_recv,
     c_send,
@@ -111,18 +129,51 @@
     for p in range(1, n_head):
         pl.semaphore_signal(barrier, inc=1, device_id=(me, head_at(p)), device_id_type=MESH)
 
-    kv[0, 0] = k_ref[...]
-    kv[0, 1] = v_ref[...]
-
+    loads = {}
+    for i, (name, src, dst) in enumerate(
+        (
+            ("k", k_hbm, kv.at[0, 0]),
+            ("v", v_hbm, kv.at[0, 1]),
+            ("doc", doc_hbm, doc_ref),
+            ("rate", rate_hbm, rate_ref),
+            ("step", step_hbm, step_ref),
+            ("w", w_hbm, w_ref),
+            ("r", r_hbm, r_ref),
+            ("x", x_hbm, x_ref),
+            ("g", g_hbm, g_ref),
+            ("gain", gain_hbm, gain_ref),
+            ("q", q_hbm, q_ref),
+            ("og", og_hbm, og_ref),
+        )
+    ):
+        loads[name] = pltpu.make_async_copy(src, dst, load_sem.at[i])
+        loads[name].start()
+
+    def loaded(*which):
+        for name in which:
+            loads[name].wait()
+
+    loaded("k", "v")
     pl.semaphore_wait(barrier, len(offsets) + n_head - 1)
 
-    kv_copies = {}
-    for d in (4, 1, 3, 2):
-        kv_copies[d] = push(
-            kv.at[0], kv.at[d], kv_send.at[d - 1], kv_recv.at[d - 1], (seq_at(d), hd)
-        )
-        kv_copies[d].start()
-
+    lane = lax.rem(me, 4)
+    kv_copies = {4: push(kv.at[0], kv.at[4], kv_send.at[3], kv_recv.at[3], (seq_at(4), hd))}
+    kv_copies[4].start()
+    for d in (1, 3, 2):
+        wraps = lane + d >= 4
+        if KV_ROW:
+            source = jnp.where(wraps, 4, 0)
+            to = me - lane + lax.rem(lane + d, 4)
+        else:
+            source, to = 0, seq_at(d)
+        copy = push(kv.at[source], kv.at[d], kv_send.at[d - 1], kv_recv.at[d - 1], (to, hd))
+        kv_copies[d] = copy
+        if KV_ROW:
+            pl.when(jnp.logical_not(wraps))(copy.start)
+        else:
+            copy.start()
+
+    loaded("doc", "rate", "step")
     base = (me * tok).astype(F32)
     lens = jnp.broadcast_to(doc_ref[...].astype(F32), (DIM, DIM))
     i0 = lax.broadcasted_iota(jnp.int32, (DIM, DIM), 0)
@@ -136,10 +187,10 @@
     fp_col = jnp.max(jnp.where(first_r <= t_col, first_r, 0.0), axis=1, keepdims=True)
     fp_last = fp_row[:, tok - 1 : tok]
 
-    sub = lax.broadcasted_iota(jnp.int32, (heads, 1), 0)
-    rate = jnp.zeros((heads, 1), F32)
-    for h in range(heads):
-        rate = jnp.where(sub == h, rate_ref[h], rate)
+    on_diag = lax.broadcasted_iota(jnp.int32, (heads, heads), 0) == lax.broadcasted_iota(
+        jnp.int32, (heads, heads), 1
+    )
+    rate = jnp.sum(jnp.where(on_diag, rate_ref[...], 0.0), axis=1, keepdims=True)
     decay = -(rate * step_ref[...])
     j0 = lax.broadcasted_iota(jnp.int32, (tok, tok), 0)
     j1 = lax.broadcasted_iota(jnp.int32, (tok, tok), 1)
@@ -168,43 +219,39 @@
         copy.start()
         c_copies.append(copy)
 
+    loaded("w", "r", "x", "g")
     wt[...] = flip(w_ref[...])
     rt[...] = flip(r_ref[...])
 
-    def part_loop(h, _):
-        scaled_w = (wt[...] * rows[1, pl.ds(h, 1), :]).astype(BF16)
-        scaled_r = (rt[...] * rows[2, pl.ds(h, 1), :]).astype(BF16)
-        st_out[0, 0, h] = nn(scaled_w, x_ref[:, cols(h)]).astype(BF16)
-        st_out[1, 0, h] = nn(scaled_r, g_ref[:, cols(h)]).astype(BF16)
-        return 0
-
-    lax.fori_loop(0, heads, part_loop, 0)
-
     pos = (lax.rem(me, 4), lax.rem(3 + SHIFT + n_seq - me, 4))
     sign = (1, -1)
-    st_copies = {}
-
-    def send_state(which, stage):
+    each = heads // CHUNKS
+
+    def state_copy(which, stage, c):
         y = pos[which]
-        if stage == 0:
-            step = 1 - 2 * lax.rem(y, 2)
-        elif stage == 1:
-            step = 3 - 2 * y
-        else:
-            step = 4
+        step = (1 - 2 * lax.rem(y, 2), 3 - 2 * y, 4)[stage]
         to = lax.rem(me + sign[which] * step + n_seq, n_seq)
-        copy = push(
-            st_out.at[which, stage],
-            st_in.at[which, stage],
-            st_send.at[which, stage],
-            st_recv.at[which, stage],
+        part = pl.ds(c * each, each)
+        return push(
+            st_out.at[which, stage, part],
+            st_in.at[which, stage, part],
+            st_send.at[which, stage, c],
+            st_recv.at[which, stage, c],
             (to, hd),
         )
-        copy.start()
-        st_copies[which, stage] = copy
-
-    send_state(0, 0)
-    send_state(1, 0)
+
+    def part_loop(c, _):
+        for k in range(each):
+            h = c * each + k
+            scaled_w = (wt[...] * rows[1, pl.ds(h, 1), :]).astype(BF16)
+            scaled_r = (rt[...] * rows[2, pl.ds(h, 1), :]).astype(BF16)
+            st_out[0, 0, h] = nn(scaled_w, x_ref[:, cols(h)]).astype(BF16)
+            st_out[1, 0, h] = nn(scaled_r, g_ref[:, cols(h)]).astype(BF16)
+        for which in (0, 1):
+            state_copy(which, 0, c).start()
+        return 0
+
+    lax.fori_loop(0, CHUNKS, part_loop, 0)
 
     tail_c = jnp.where(fp_col == fp_last, jnp.exp(total_r - run_c), 0.0)
     lead_c = jnp.where(fp_col < base, jnp.exp(run_c), 0.0)
@@ -214,6 +261,8 @@
         lead_col[h] = lead_c[:, h : h + 1]
 
     cross = nt(w_ref[...], r_ref[...])
+    loaded("gain", "q", "og")
+    head_lane = lax.broadcasted_iota(jnp.int32, (1, heads), 1)
     keep = (j0 <= j1) & (fp_col == fp_row)
     w_acc[...] = jnp.zeros_like(w_acc)
 
@@ -223,8 +272,9 @@
         corr = nt(x_h, g_h)
         dec = jnp.exp(jnp.where(keep, rows[0, pl.ds(h, 1), :] - run_col[h], NEG))
         w_acc[...] += corr * dec
+        gain = jnp.sum(jnp.where(head_lane == h, gain_ref[...], 0.0), axis=1, keepdims=True)
         mix = (cross * dec).astype(BF16)
-        gi_acc[:, cols(h)] = nn(mix, g_h) + gain_ref[h] * g_h.astype(F32)
+        gi_acc[:, cols(h)] = nn(mix, g_h) + gain * g_h.astype(F32)
         return 0
 
     lax.fori_loop(0, heads, local_loop, 0)
@@ -234,6 +284,11 @@
     for c in range(n_head):
         tot[c, 0] = gw[c * (tok // n_head) : (c + 1) * (tok // n_head)]
         tot[c, 1] = gr[c * (tok // n_head) : (c + 1) * (tok // n_head)]
+
+    if KV_ROW:
+        kv_copies[4].wait_recv()
+        for d in (1, 3, 2):
+            pl.when(lane + d >= 4)(kv_copies[d].start)
 
     for copy in c_copies:
         copy.wait_recv()
@@ -256,29 +311,33 @@
     def factor(which, i, h):
         return coef[which, i, pl.ds(h, 1), :]
 
-    for which in (0, 1):
-        st_copies[which, 0].wait_recv()
-
-        def pair_loop(h, _, which=which):
-            st_out[which, 1, h] = (
-                factor(which, 0, h) * st_out[which, 0, h].astype(F32)
-                + factor(which, 1, h) * st_in[which, 0, h].astype(F32)
-            ).astype(BF16)
-            return 0
-
-        lax.fori_loop(0, heads, pair_loop, 0)
-        send_state(which, 1)
-
-    for d in (4, 1, 3, 2):
+    def pair_loop(c, _):
+        for which in (0, 1):
+            state_copy(which, 0, c).wait_recv()
+            for k in range(each):
+                h = c * each + k
+                st_out[which, 1, h] = (
+                    factor(which, 0, h) * st_out[which, 0, h].astype(F32)
+                    + factor(which, 1, h) * st_in[which, 0, h].astype(F32)
+                ).astype(BF16)
+            state_copy(which, 1, c).start()
+        return 0
+
+    lax.fori_loop(0, CHUNKS, pair_loop, 0)
+
+    for i in range(q_heads):
+        q_rows[i * tok : (i + 1) * tok] = q_ref[:, i * DIM : (i + 1) * DIM]
+        og_rows[i * tok : (i + 1) * tok] = og_ref[:, i * DIM : (i + 1) * DIM]
+    for d in (1, 3, 2) if KV_ROW else (4, 1, 3, 2):
         kv_copies[d].wait_recv()
     for o in range(REACH + 1):
         kt[o] = flip(kv[o, 0]).astype(BF16)
-    dacc[...] = jnp.zeros_like(dacc)
     spot = lax.broadcasted_iota(jnp.int32, (tok, 1), 0).astype(F32)
 
-    def attend(i, _):
+    def attend(i):
         q_i = q_ref[:, cols(i)]
         og_i = og_ref[:, cols(i)]
+        here = pl.ds(pl.multiple_of(i * tok, tok), tok)
         scores = []
         for o in range(REACH + 1):
             key_pos = spot + (base - float(o * tok))
@@ -304,45 +363,46 @@
         dq = jnp.zeros((DIM, tok), F32)
         for o in range(REACH + 1):
             ds = (probs[o] * (dprob[o] - delta)).astype(BF16)
-            dacc[o, 0] += nn(ds, q_i)
-            dacc[o, 1] += nn(halves[o], og_i)
+            ds_all[o, :, here] = ds
+            ph_all[o, :, here] = halves[o]
             dq += nn(kt[o], ds)
         gq_ref[:, cols(i)] = (jnp.transpose(dq) * SCALE).astype(BF16)
+
+    def attend_loop(c, _):
+        attend(c)
+        for which in (0, 1):
+            state_copy(which, 1, c).wait_recv()
+            first = 1 - lax.rem(pos[which], 2)
+            for k in range(each):
+                h = c * each + k
+                st_out[which, 2, h] = (
+                    factor(which, 2, h) * st_out[which, first, h].astype(F32)
+                    + factor(which, 3, h) * st_in[which, 1, h].astype(F32)
+                ).astype(BF16)
+            state_copy(which, 2, c).start()
         return 0
 
-    lax.fori_loop(0, q_heads // 2, attend, 0)
-
-    for which in (0, 1):
-        st_copies[which, 1].wait_recv()
-        base_at = 1 - lax.rem(pos[which], 2)
-
-        def reach_loop(h, _, which=which, base_at=base_at):
-            st_out[which, 2, h] = (
-                factor(which, 2, h) * st_out[which, base_at, h].astype(F32)
-                + factor(which, 3, h) * st_in[which, 1, h].astype(F32)
-            ).astype(BF16)
-            return 0
-
-        lax.fori_loop(0, heads, reach_loop, 0)
-        send_state(which, 2)
-
-    lax.fori_loop(q_heads // 2, q_heads, attend, 0)
-
-    dkv_copies = {}
-    for d in (4, 2, 3, 1):
-        dkv_out[d - 1, 0] = (dacc[d, 0] * SCALE).astype(BF16)
-        dkv_out[d - 1, 1] = dacc[d, 1].astype(BF16)
-        dkv_copies[d] = push(
+    lax.fori_loop(0, CHUNKS, attend_loop, 0)
+
+    def dkv_copy(d):
+        return push(
             dkv_out.at[d - 1],
             dkv_in.at[d - 1],
             dkv_send.at[d - 1],
             dkv_recv.at[d - 1],
-            (seq_at(-d), hd),
+            (lax.rem(me - d + n_seq, n_seq), hd),
         )
-        dkv_copies[d].start()
-
-    for which in (0, 1):
-        st_copies[which, 2].wait_recv()
+
+    def grad_loop(step, _):
+        d = REACH - step
+        dkv_out[d - 1, 0] = (nn(ds_all[d], q_rows[...]) * SCALE).astype(BF16)
+        dkv_out[d - 1, 1] = nn(ph_all[d], og_rows[...]).astype(BF16)
+        dkv_copy(d).start()
+        return 0
+
+    lax.fori_loop(0, REACH, grad_loop, 0)
+    own_grad[0] = nn(ds_all[0], q_rows[...]) * SCALE
+    own_grad[1] = nn(ph_all[0], og_rows[...])
 
     def arrived(which, h):
         return (
@@ -351,34 +411,41 @@
             + factor(which, 6, h) * st_in[which, 2, h].astype(F32)
         ).astype(BF16)
 
-    def carry_loop(h, sums):
-        state, adjoint = arrived(0, h), arrived(1, h)
-        x_h = x_ref[:, cols(h)]
-        g_h = g_ref[:, cols(h)]
-        tail_h, lead_h = tail_col[h], lead_col[h]
-        gi_ref[:, cols(h)] = (gi_acc[:, cols(h)] + nn(w_ref[...], adjoint) * tail_h).astype(BF16)
-        return (
-            sums[0] + nt(x_h, adjoint) * tail_h,
-            sums[1] + nt(g_h, state) * lead_h,
-        )
+    def carry_loop(c, sums):
+        gw, gr = sums
+        for which in (0, 1):
+            state_copy(which, 2, c).wait_recv()
+        for k in range(each):
+            h = c * each + k
+            state, adjoint = arrived(0, h), arrived(1, h)
+            x_h = x_ref[:, cols(h)]
+            g_h = g_ref[:, cols(h)]
+            tail_h, lead_h = tail_col[h], lead_col[h]
+            gi_ref[:, cols(h)] = (
+                gi_acc[:, cols(h)] + nn(w_ref[...], adjoint) * tail_h
+            ).astype(BF16)
+            gw += nt(x_h, adjoint) * tail_h
+            gr += nt(g_h, state) * lead_h
+        return gw, gr
 
     zeros = jnp.zeros((tok, DIM), F32)
-    gw, gr = lax.fori_loop(0, heads, carry_loop, (zeros, zeros))
+    gw, gr = lax.fori_loop(0, CHUNKS, carry_loop, (zeros, zeros))
     rows_each = tok // n_head
     for c in range(n_head):
-        tot[c, 0] += gw[c * rows_each : (c + 1) * rows_each]
-        tot[c, 1] += gr[c * rows_each : (c + 1) * rows_each]
+        for i, total in enumerate((gw, gr)):
+            part = tot[c, i] + total[c * rows_each : (c + 1) * rows_each]
+            tot[c, i] = part
+            rs_out[c, i] = part.astype(BF16)
     rs_copies = []
     for p in range(1, n_head):
         to = head_at(p)
-        copy = push(tot.at[to], rs_in.at[p - 1], rs_send.at[p - 1], rs_recv.at[p - 1], (me, to))
+        copy = push(rs_out.at[to], rs_in.at[p - 1], rs_send.at[p - 1], rs_recv.at[p - 1], (me, to))
         copy.start()
         rs_copies.append(copy)
 
-    gk = dacc[0, 0] * SCALE
-    gv = dacc[0, 1]
-    for d in (4, 2, 3, 1):
-        dkv_copies[d].wait_recv()
+    gk, gv = own_grad[0], own_grad[1]
+    for d in (4, 3, 2, 1):
+        dkv_copy(d).wait_recv()
         gk += dkv_in[d - 1, 0].astype(F32)
         gv += dkv_in[d - 1, 1].astype(F32)
     gk_ref[...] = gk.astype(BF16)
@@ -388,8 +455,8 @@
     gr_out = tot[hd, 1]
     for p in range(1, n_head):
         rs_copies[p - 1].wait_recv()
-        gw_out += rs_in[p - 1, 0]
-        gr_out += rs_in[p - 1, 1]
+        gw_out += rs_in[p - 1, 0].astype(F32)
+        gr_out += rs_in[p - 1, 1].astype(F32)
     gw_ref[...] = gw_out
     gr_ref[...] = gr_out
 
@@ -397,25 +464,56 @@
         copy.wait_send()
     for copy in c_copies:
         copy.wait_send()
-    for copy in st_copies.values():
-        copy.wait_send()
-    for copy in dkv_copies.values():
-        copy.wait_send()
+
+    def drain(c, _):
+        for which in (0, 1):
+            for stage in range(3):
+                state_copy(which, stage, c).wait_send()
+        dkv_copy(c + 1).wait_send()
+        return 0
+
+    lax.fori_loop(0, CHUNKS, drain, 0)
     for copy in rs_copies:
         copy.wait_send()
+
+
+def store(*refs):
+    *refs, sem = refs
+    count = len(refs) // 2
+    copies = [
+        pltpu.make_async_copy(refs[i], refs[count + i], sem.at[i]) for i in range(count)
+    ]
+    for copy in copies:
+        copy.start()
+    for copy in copies:
+        copy.wait()
 
 
 def on_device(n_seq, n_head, *args):
     (x, g, w, r, step, rate, gain, q, k, v, og, docs) = args
     tok, heads = x.shape[0], step.shape[0]
     vmem = pl.BlockSpec(memory_space=pltpu.VMEM)
-    smem = pl.BlockSpec(memory_space=pltpu.SMEM)
+    hbm = pl.BlockSpec(memory_space=pltpu.HBM)
     rows_each = tok // n_head
     dma = pltpu.SemaphoreType.DMA
     scratch = [
+        pltpu.VMEM(x.shape, BF16),
+        pltpu.VMEM(g.shape, BF16),
+        pltpu.VMEM(w.shape, BF16),
+        pltpu.VMEM(r.shape, BF16),
+        pltpu.VMEM(step.shape, F32),
+        pltpu.VMEM((1, heads), F32),
+        pltpu.VMEM((1, heads), F32),
+        pltpu.VMEM(q.shape, BF16),
+        pltpu.VMEM(og.shape, BF16),
+        pltpu.VMEM((1, docs.shape[0]), jnp.int32),
         pltpu.VMEM((REACH + 1, 2, tok, DIM), BF16),
         pltpu.VMEM((REACH + 1, DIM, tok), BF16),
-        pltpu.VMEM((REACH + 1, 2, tok, DIM), F32),
+        pltpu.VMEM((q.shape[1] // DIM * tok, DIM), BF16),
+        pltpu.VMEM((q.shape[1] // DIM * tok, DIM), BF16),
+        pltpu.VMEM((REACH + 1, tok, q.shape[1] // DIM * tok), BF16),
+        pltpu.VMEM((REACH + 1, tok, q.shape[1] // DIM * tok), BF16),
+        pltpu.VMEM((2, tok, DIM), F32),
         pltpu.VMEM((REACH, 2, tok, DIM), BF16),
         pltpu.VMEM((REACH, 2, tok, DIM), BF16),
         pltpu.VMEM((7, heads, DIM), F32),
@@ -431,19 +529,21 @@
         pltpu.VMEM((tok, tok), F32),
         pltpu.VMEM((2, 7, heads, DIM), F32),
         pltpu.VMEM((n_head, 2, rows_each, DIM), F32),
-        pltpu.VMEM((n_head - 1, 2, rows_each, DIM), F32),
+        pltpu.VMEM((n_head, 2, rows_each, DIM), BF16),
+        pltpu.VMEM((n_head - 1, 2, rows_each, DIM), BF16),
+        dma((len(args),)),
         dma((REACH,)),
         dma((REACH,)),
         dma((6,)),
         dma((7,)),
-        dma((2, 3)),
-        dma((2, 3)),
+        dma((2, 3, CHUNKS)),
+        dma((2, 3, CHUNKS)),
         dma((REACH,)),
         dma((REACH,)),
         dma((n_head - 1,)),
         dma((n_head - 1,)),
     ]
-    return pl.pallas_call(
+    made = pl.pallas_call(
         functools.partial(kernel, n_seq, n_head),
         out_shape=(
             jax.ShapeDtypeStruct(x.shape, BF16),
@@ -453,13 +553,21 @@
             jax.ShapeDtypeStruct(k.shape, BF16),
             jax.ShapeDtypeStruct(v.shape, BF16),
         ),
-        in_specs=[vmem] * 5 + [smem] * 2 + [vmem] * 5,
+        in_specs=[hbm] * len(args),
         out_specs=(vmem,) * 6,
         scratch_shapes=scratch,
         compiler_params=pltpu.CompilerParams(
             collective_id=0, has_side_effects=True, vmem_limit_bytes=48 * 2**20
         ),
-    )(x, g, w, r, step, rate, gain, q, k, v, og, docs.reshape(1, -1))
+    )(*[pltpu.with_memory_space_constraint(a, pltpu.HBM) for a in (x, g, w, r, step, rate.reshape(1, -1), gain.reshape(1, -1), q, k, v, og, docs.reshape(1, -1))])
+    return pl.pallas_call(
+        store,
+        out_shape=[jax.ShapeDtypeStruct(m.shape, m.dtype) for m in made],
+        in_specs=[vmem] * len(made),
+        out_specs=[hbm] * len(made),
+        scratch_shapes=[dma((len(made),))],
+        compiler_params=pltpu.CompilerParams(vmem_limit_bytes=2 * 2**20),
+    )(*made)
 
 
 def solution(mesh):

time: 67.6 us -> 49.4 us (0.73)
  the two profiles are of different devices: /device:TPU:1 before, /device:TPU:120 now
where the time goes in v2:
time: 49.4 us; the launch traced here: 49.3 us
  Pallas kernels  48.6 us (98%)
  between operations  0.64 us (1%)
    pallas_call x1, Pallas kernels, on_device(): pl.pallas_call(functools.partial(kernel, n_seq, n_head), out_shape=(jax.S...  47.7 us

profile of v2, /device:TPU:120, one launch (start us, length us, event | category | flops | bytes accessed | tf_op | source)
XLA Modules:
  0.0 49.3 jit_solution(14253317064295378572)
XLA Ops:
  0.6 47.7 %shard_map.163 = (bf16[256,1024]{1,0:T(8,128)(2,1)S(1)}, f32[32,128]{1,0:T(8,128)S(1)}, f32[32,128]{1,0:T(8,128)S(1)}, bf16[256,512]{1,0:T(8,128)(2,1)S(1)}, bf1...) custom-call(bf16[256,1024]{1,0:T(8,128)(2,1)} %x_hbm.1, bf16[256,1024]{1,0:T(8,128)(2,1)} %g_hbm.1, ...), custom_call_target="tpu_custom_call" | custom-call | tf_op jit(solution)/shard_map/pallas_call | solution.py:546
  48.3 1.0 %shard_map.164 = (bf16[256,1024]{1,0:T(8,128)(2,1)}, f32[32,128]{1,0:T(8,128)}, f32[32,128]{1,0:T(8,128)}, bf16[256,512]{1,0:T(8,128)(2,1)}, bf16[256,128]{1,0:T(8,128)(2,1)}, /*index=5*/bf16[256,128]{1,0:T(8,128)(2,1)}) custom-call(bf16[256,1024]{1,0:T(8,128)(2,1)S(1)} %get-tuple-element.12.refs_0_, f32[32,128]{1,0:T(8,128)S(1)} %get-tuple-element.13.refs_1_, ...), custom_call_target="tpu_custom_call" | custom-call | tf_op jit(solution)/shard_map/pallas_call | solution.py:563

commit v3 on v2

--- a/solution.py
+++ b/solution.py
@@ -14,9 +14,8 @@
 NEG = -1e30
 SCALE = DIM ** (-0.5)
 SCALE2 = SCALE * math.log2(math.e)
-SHIFT = 1
 CHUNKS = 4
-KV_ROW = True
+ORDER = 0
 
 F32 = jnp.float32
 BF16 = jnp.bfloat16
@@ -73,6 +72,11 @@
     kt,
     q_rows,
     og_rows,
+    s_all,
+    dp_all,
+    row_norm,
+    row_delta,
+    dq_acc,
     ds_all,
     ph_all,
     own_grad,
@@ -114,6 +118,12 @@
     def seq_at(d):
         return lax.rem(me + (d + n_seq), n_seq)
 
+    def exists(d):
+        return (me + d >= 0) & (me + d < n_seq)
+
+    def absent(d):
+        return jnp.logical_not(exists(d))
+
     def head_at(p):
         return lax.rem(hd + p, n_head)
 
@@ -124,8 +134,15 @@
 
     barrier = pltpu.get_barrier_semaphore()
     offsets = [d for d in range(-REACH, REACH + 1) if d]
+    peers = n_head - 1
     for d in offsets:
-        pl.semaphore_signal(barrier, inc=1, device_id=(seq_at(d), hd), device_id_type=MESH)
+        there = exists(d)
+        peers += there.astype(jnp.int32)
+
+        @pl.when(there)
+        def _(d=d):
+            pl.semaphore_signal(barrier, inc=1, device_id=(seq_at(d), hd), device_id_type=MESH)
+
     for p in range(1, n_head):
         pl.semaphore_signal(barrier, inc=1, device_id=(me, head_at(p)), device_id_type=MESH)
 
@@ -152,26 +169,6 @@
     def loaded(*which):
         for name in which:
             loads[name].wait()
-
-    loaded("k", "v")
-    pl.semaphore_wait(barrier, len(offsets) + n_head - 1)
-
-    lane = lax.rem(me, 4)
-    kv_copies = {4: push(kv.at[0], kv.at[4], kv_send.at[3], kv_recv.at[3], (seq_at(4), hd))}
-    kv_copies[4].start()
-    for d in (1, 3, 2):
-        wraps = lane + d >= 4
-        if KV_ROW:
-            source = jnp.where(wraps, 4, 0)
-            to = me - lane + lax.rem(lane + d, 4)
-        else:
-            source, to = 0, seq_at(d)
-        copy = push(kv.at[source], kv.at[d], kv_send.at[d - 1], kv_recv.at[d - 1], (to, hd))
-        kv_copies[d] = copy
-        if KV_ROW:
-            pl.when(jnp.logical_not(wraps))(copy.start)
-        else:
-            copy.start()
 
     loaded("doc", "rate", "step")
     base = (me * tok).astype(F32)
@@ -213,31 +210,73 @@
     rows[1] = jnp.where(fp_row == fp_last, jnp.exp(total_c - run_r), 0.0)
     rows[2] = jnp.where(fp_row < base, jnp.exp(run_r), 0.0)
     cbuf[3] = jnp.broadcast_to(jnp.where(fp_last < base, jnp.exp(total_c), 0.0), (heads, DIM))
-    c_copies = []
-    for i, d in enumerate((-3, -2, -1, 1, 2, 3)):
-        copy = push(cbuf.at[3], cbuf.at[3 - d], c_send.at[i], c_recv.at[3 - d], (seq_at(d), hd))
-        copy.start()
-        c_copies.append(copy)
+
+    loaded("k", "v")
+    pl.semaphore_wait(barrier, peers)
+    kv_copies = {}
+    for d in (4, 1, 3, 2):
+        kv_copies[d] = push(
+            kv.at[0], kv.at[d], kv_send.at[d - 1], kv_recv.at[d - 1], (seq_at(d), hd)
+        )
+        pl.when(exists(d))(kv_copies[d].start)
+    c_copies = {}
+    for d in (-3, -2, -1, 1, 2, 3):
+        c_copies[d] = push(
+            cbuf.at[3], cbuf.at[3 - d], c_send.at[d + 3], c_recv.at[3 - d], (seq_at(d), hd)
+        )
+        pl.when(exists(d))(c_copies[d].start)
+
+        @pl.when(absent(d))
+        def _(d=d):
+            cbuf[3 + d] = jnp.zeros_like(cbuf[3 + d])
+
+    for d in range(1, REACH + 1):
+
+        @pl.when(absent(-d))
+        def _(d=d):
+            kv[d] = jnp.zeros_like(kv[d])
+
+        @pl.when(absent(d))
+        def _(d=d):
+            dkv_in[d - 1] = jnp.zeros_like(dkv_in[d - 1])
+
+    parity = lax.rem(me, 2)
+    later = (parity == 1, parity == 0)
+    sign = (1, -1)
+    ahead = [jnp.where(later[w], sign[w], 3 * sign[w]) for w in (0, 1)]
+    behind = [jnp.where(later[w], -3 * sign[w], -sign[w]) for w in (0, 1)]
+    sends = [(None, exists(ahead[w]), exists(4 * sign[w])) for w in (0, 1)]
+    gets = [(None, exists(behind[w]), exists(-4 * sign[w])) for w in (0, 1)]
+
+    def when(condition, do):
+        if condition is None:
+            do()
+        else:
+            pl.when(condition)(do)
+
+    for which in (0, 1):
+        for stage in (1, 2):
+
+            @pl.when(jnp.logical_not(gets[which][stage]))
+            def _(which=which, stage=stage):
+                st_in[which, stage] = jnp.zeros_like(st_in[which, stage])
 
     loaded("w", "r", "x", "g")
     wt[...] = flip(w_ref[...])
     rt[...] = flip(r_ref[...])
 
-    pos = (lax.rem(me, 4), lax.rem(3 + SHIFT + n_seq - me, 4))
-    sign = (1, -1)
     each = heads // CHUNKS
 
     def state_copy(which, stage, c):
-        y = pos[which]
-        step = (1 - 2 * lax.rem(y, 2), 3 - 2 * y, 4)[stage]
-        to = lax.rem(me + sign[which] * step + n_seq, n_seq)
+        step = (1 - 2 * parity, ahead[which], 4 * sign[which])[stage]
+        source = (0, 1, jnp.where(later[which], 0, 1))[stage]
         part = pl.ds(c * each, each)
         return push(
-            st_out.at[which, stage, part],
+            st_out.at[which, source, part],
             st_in.at[which, stage, part],
             st_send.at[which, stage, c],
             st_recv.at[which, stage, c],
-            (to, hd),
+            (lax.rem(me + step + n_seq, n_seq), hd),
         )
 
     def part_loop(c, _):
@@ -249,6 +288,7 @@
             st_out[1, 0, h] = nn(scaled_r, g_ref[:, cols(h)]).astype(BF16)
         for which in (0, 1):
             state_copy(which, 0, c).start()
+            pl.when(later[which] & sends[which][2])(state_copy(which, 2, c).start)
         return 0
 
     lax.fori_loop(0, CHUNKS, part_loop, 0)
@@ -278,40 +318,23 @@
         return 0
 
     lax.fori_loop(0, heads, local_loop, 0)
-    w_sum = w_acc[...]
-    gw = nn(w_sum.astype(BF16), r_ref[...])
-    gr = nn(flip(w_sum).astype(BF16), w_ref[...])
-    for c in range(n_head):
-        tot[c, 0] = gw[c * (tok // n_head) : (c + 1) * (tok // n_head)]
-        tot[c, 1] = gr[c * (tok // n_head) : (c + 1) * (tok // n_head)]
-
-    if KV_ROW:
-        kv_copies[4].wait_recv()
-        for d in (1, 3, 2):
-            pl.when(lane + d >= 4)(kv_copies[d].start)
-
-    for copy in c_copies:
-        copy.wait_recv()
+    for d, copy in c_copies.items():
+        pl.when(exists(-d))(copy.wait_recv)
     for which in (0, 1):
-        y, s = pos[which], sign[which]
-        c0, c1, c2, c3 = [cbuf[3 + s * (q - y)] for q in range(4)]
-        own, after = cbuf[3], cbuf[3 + s]
-        odd = lax.rem(y, 2) == 1
+        s = sign[which]
+        c1, c2, c3 = [cbuf[3 - s * k] for k in (1, 2, 3)]
+        own, partner = cbuf[3], cbuf[3 + s]
         one, zero = jnp.ones_like(own), jnp.zeros_like(own)
-        coef[which, 0] = jnp.where(odd, one, after)
-        coef[which, 1] = jnp.where(odd, own, one)
-        coef[which, 2] = jnp.where(y < 2, c2 * c3, one)
-        coef[which, 3] = jnp.where(y < 2, one, zero)
-        coef[which, 4] = jnp.where(odd, one, zero)
-        coef[which, 5] = jnp.where(y == 2, one, jnp.where(y == 3, c2, zero))
-        coef[which, 6] = jnp.where(
-            y == 0, one, jnp.where(y == 1, c0, jnp.where(y == 2, c0 * c1, c0 * c1 * c2))
-        )
+        coef[which, 0] = jnp.where(later[which], one, partner)
+        coef[which, 1] = jnp.where(later[which], own, one)
+        coef[which, 2] = jnp.where(later[which], one, zero)
+        coef[which, 3] = jnp.where(later[which], c1, one)
+        coef[which, 4] = jnp.where(later[which], c1 * c2 * c3, c1 * c2)
 
     def factor(which, i, h):
         return coef[which, i, pl.ds(h, 1), :]
 
-    def pair_loop(c, _):
+    def pair_step(c, _=0):
         for which in (0, 1):
             state_copy(which, 0, c).wait_recv()
             for k in range(each):
@@ -320,67 +343,91 @@
                     factor(which, 0, h) * st_out[which, 0, h].astype(F32)
                     + factor(which, 1, h) * st_in[which, 0, h].astype(F32)
                 ).astype(BF16)
-            state_copy(which, 1, c).start()
+            when(sends[which][1], state_copy(which, 1, c).start)
+            pl.when(jnp.logical_not(later[which]) & sends[which][2])(state_copy(which, 2, c).start)
         return 0
-
-    lax.fori_loop(0, CHUNKS, pair_loop, 0)
 
     for i in range(q_heads):
         q_rows[i * tok : (i + 1) * tok] = q_ref[:, i * DIM : (i + 1) * DIM]
         og_rows[i * tok : (i + 1) * tok] = og_ref[:, i * DIM : (i + 1) * DIM]
-    for d in (1, 3, 2) if KV_ROW else (4, 1, 3, 2):
-        kv_copies[d].wait_recv()
-    for o in range(REACH + 1):
+    spot = lax.broadcasted_iota(jnp.int32, (tok, 1), 0).astype(F32)
+
+    def head_lanes(i):
+        return pl.ds(pl.multiple_of(i * tok, tok), tok)
+
+    def score_step(o):
         kt[o] = flip(kv[o, 0]).astype(BF16)
-    spot = lax.broadcasted_iota(jnp.int32, (tok, 1), 0).astype(F32)
-
-    def attend(i):
-        q_i = q_ref[:, cols(i)]
-        og_i = og_ref[:, cols(i)]
-        here = pl.ds(pl.multiple_of(i * tok, tok), tok)
-        scores = []
-        for o in range(REACH + 1):
+
+        def one_head(i, _):
             key_pos = spot + (base - float(o * tok))
             allowed = key_pos >= fp_row
             if o == 0:
                 allowed = allowed & (key_pos <= t_row)
-            scores.append(jnp.where(allowed, nt(kv[o, 0], q_i) * SCALE2, NEG))
+            s_all[o, :, head_lanes(i)] = jnp.where(
+                allowed, nt(kv[o, 0], q_ref[:, cols(i)]) * SCALE2, NEG
+            )
+            dp_all[o, :, head_lanes(i)] = nt(kv[o, 1], og_ref[:, cols(i)])
+            return 0
+
+        lax.fori_loop(0, q_heads, one_head, 0)
+
+    def softmax_step(i):
+        here = head_lanes(i)
+        blocks = range(REACH + 1)
+        scores = [s_all[o, :, here] for o in blocks]
         top = functools.reduce(jnp.maximum, [jnp.max(s, axis=0, keepdims=True) for s in scores])
         weights = [jnp.exp2(s - top) for s in scores]
+        for o in blocks:
+            s_all[o, :, here] = weights[o]
         norm = 1.0 / functools.reduce(
             jnp.add, [jnp.sum(e, axis=0, keepdims=True) for e in weights]
         )
-        probs = [e * norm for e in weights]
-        halves = [p.astype(BF16) for p in probs]
-        dprob = [nt(kv[o, 1], og_i) for o in range(REACH + 1)]
-        delta = functools.reduce(
+        row_norm[:, here] = norm
+        row_delta[:, here] = norm * functools.reduce(
             jnp.add,
-            [
-                jnp.sum(halves[o].astype(F32) * dprob[o], axis=0, keepdims=True)
-                for o in range(REACH + 1)
-            ],
-        )
-        dq = jnp.zeros((DIM, tok), F32)
-        for o in range(REACH + 1):
-            ds = (probs[o] * (dprob[o] - delta)).astype(BF16)
-            ds_all[o, :, here] = ds
-            ph_all[o, :, here] = halves[o]
-            dq += nn(kt[o], ds)
-        gq_ref[:, cols(i)] = (jnp.transpose(dq) * SCALE).astype(BF16)
+            [jnp.sum(weights[o] * dp_all[o, :, here], axis=0, keepdims=True) for o in blocks],
+        )
+
+    def grad_step(d):
+        def one_head(i, _):
+            here = head_lanes(i)
+            prob = s_all[d, :, here] * row_norm[:, here]
+            ds = (prob * (dp_all[d, :, here] - row_delta[:, here])).astype(BF16)
+            ds_all[d, :, here] = ds
+            ph_all[d, :, here] = prob.astype(BF16)
+            dq_acc[i] += nn(kt[d], ds)
+            return 0
+
+        lax.fori_loop(0, q_heads, one_head, 0)
+
+    def kv_step(d):
+        pl.when(exists(-d))(kv_copies[d].wait_recv)
+        score_step(d)
+
+    score_step(0)
+    for d, c in zip((4, 1, 3, 2), range(CHUNKS)):
+        if ORDER == 0:
+            pair_step(c)
+            kv_step(d)
+        elif ORDER == 1:
+            kv_step(d)
+            pair_step(c)
+        elif ORDER == 2:
+            if c < 2:
+                pair_step(2 * c)
+                pair_step(2 * c + 1)
+            kv_step(d)
+        else:
+            kv_step(d)
+            if c >= 2:
+                pair_step(2 * c - 4)
+                pair_step(2 * c - 3)
 
     def attend_loop(c, _):
-        attend(c)
-        for which in (0, 1):
-            state_copy(which, 1, c).wait_recv()
-            first = 1 - lax.rem(pos[which], 2)
-            for k in range(each):
-                h = c * each + k
-                st_out[which, 2, h] = (
-                    factor(which, 2, h) * st_out[which, first, h].astype(F32)
-                    + factor(which, 3, h) * st_in[which, 1, h].astype(F32)
-                ).astype(BF16)
-            state_copy(which, 2, c).start()
+        softmax_step(c)
         return 0
+
+    dq_acc[...] = jnp.zeros_like(dq_acc)
 
     lax.fori_loop(0, CHUNKS, attend_loop, 0)
 
@@ -395,26 +442,37 @@
 
     def grad_loop(step, _):
         d = REACH - step
+        grad_step(d)
         dkv_out[d - 1, 0] = (nn(ds_all[d], q_rows[...]) * SCALE).astype(BF16)
         dkv_out[d - 1, 1] = nn(ph_all[d], og_rows[...]).astype(BF16)
-        dkv_copy(d).start()
+        pl.when(me >= d)(dkv_copy(d).start)
         return 0
 
     lax.fori_loop(0, REACH, grad_loop, 0)
+    grad_step(0)
+    for i in range(q_heads):
+        gq_ref[:, i * DIM : (i + 1) * DIM] = (jnp.transpose(dq_acc[i]) * SCALE).astype(BF16)
     own_grad[0] = nn(ds_all[0], q_rows[...]) * SCALE
     own_grad[1] = nn(ph_all[0], og_rows[...])
+    w_sum = w_acc[...]
+    gw = nn(w_sum.astype(BF16), r_ref[...])
+    gr = nn(flip(w_sum).astype(BF16), w_ref[...])
+    for c in range(n_head):
+        tot[c, 0] = gw[c * (tok // n_head) : (c + 1) * (tok // n_head)]
+        tot[c, 1] = gr[c * (tok // n_head) : (c + 1) * (tok // n_head)]
 
     def arrived(which, h):
         return (
-            factor(which, 4, h) * st_in[which, 0, h].astype(F32)
-            + factor(which, 5, h) * st_in[which, 1, h].astype(F32)
-            + factor(which, 6, h) * st_in[which, 2, h].astype(F32)
+            factor(which, 2, h) * st_in[which, 0, h].astype(F32)
+            + factor(which, 3, h) * st_in[which, 1, h].astype(F32)
+            + factor(which, 4, h) * st_in[which, 2, h].astype(F32)
         ).astype(BF16)
 
     def carry_loop(c, sums):
         gw, gr = sums
         for which in (0, 1):
-            state_copy(which, 2, c).wait_recv()
+            for stage in (1, 2):
+                pl.when(gets[which][stage])(state_copy(which, stage, c).wait_recv)
         for k in range(each):
             h = c * each + k
             state, adjoint = arrived(0, h), arrived(1, h)
@@ -445,7 +503,7 @@
 
     gk, gv = own_grad[0], own_grad[1]
     for d in (4, 3, 2, 1):
-        dkv_copy(d).wait_recv()
+        pl.when(exists(d))(dkv_copy(d).wait_recv)
         gk += dkv_in[d - 1, 0].astype(F32)
         gv += dkv_in[d - 1, 1].astype(F32)
     gk_ref[...] = gk.astype(BF16)
@@ -460,19 +518,20 @@
     gw_ref[...] = gw_out
     gr_ref[...] = gr_out
 
-    for copy in kv_copies.values():
-        copy.wait_send()
-    for copy in c_copies:
-        copy.wait_send()
+    for d, copy in kv_copies.items():
+        pl.when(exists(d))(copy.wait_send)
+    for d, copy in c_copies.items():
+        pl.when(exists(d))(copy.wait_send)
 
     def drain(c, _):
         for which in (0, 1):
             for stage in range(3):
-                state_copy(which, stage, c).wait_send()
-        dkv_copy(c + 1).wait_send()
+                when(sends[which][stage], state_copy(which, stage, c).wait_send)
+        pl.when(me > c)(dkv_copy(c + 1).wait_send)
         return 0
 
     lax.fori_loop(0, CHUNKS, drain, 0)
+
     for copy in rs_copies:
         copy.wait_send()
 
@@ -511,13 +570,18 @@
         pltpu.VMEM((REACH + 1, DIM, tok), BF16),
         pltpu.VMEM((q.shape[1] // DIM * tok, DIM), BF16),
         pltpu.VMEM((q.shape[1] // DIM * tok, DIM), BF16),
+        pltpu.VMEM((REACH + 1, tok, q.shape[1] // DIM * tok), F32),
+        pltpu.VMEM((REACH + 1, tok, q.shape[1] // DIM * tok), F32),
+        pltpu.VMEM((1, q.shape[1] // DIM * tok), F32),
+        pltpu.VMEM((1, q.shape[1] // DIM * tok), F32),
+        pltpu.VMEM((q.shape[1] // DIM, DIM, tok), F32),
         pltpu.VMEM((REACH + 1, tok, q.shape[1] // DIM * tok), BF16),
         pltpu.VMEM((REACH + 1, tok, q.shape[1] // DIM * tok), BF16),
         pltpu.VMEM((2, tok, DIM), F32),
         pltpu.VMEM((REACH, 2, tok, DIM), BF16),
         pltpu.VMEM((REACH, 2, tok, DIM), BF16),
         pltpu.VMEM((7, heads, DIM), F32),
-        pltpu.VMEM((2, 3, heads, DIM, DIM), BF16),
+        pltpu.VMEM((2, 2, heads, DIM, DIM), BF16),
         pltpu.VMEM((2, 3, heads, DIM, DIM), BF16),
         pltpu.VMEM((DIM, tok), F32),
         pltpu.VMEM((DIM, tok), F32),
@@ -527,14 +591,14 @@
         pltpu.VMEM((heads, tok, 1), F32),
         pltpu.VMEM((tok, heads * DIM), F32),
         pltpu.VMEM((tok, tok), F32),
-        pltpu.VMEM((2, 7, heads, DIM), F32),
+        pltpu.VMEM((2, 5, heads, DIM), F32),
         pltpu.VMEM((n_head, 2, rows_each, DIM), F32),
         pltpu.VMEM((n_head, 2, rows_each, DIM), BF16),
         pltpu.VMEM((n_head - 1, 2, rows_each, DIM), BF16),
         dma((len(args),)),
         dma((REACH,)),
         dma((REACH,)),
-        dma((6,)),
+        dma((7,)),
         dma((7,)),
         dma((2, 3, CHUNKS)),
         dma((2, 3, CHUNKS)),

time: 49.4 us -> 45.9 us (0.929)
  Pallas kernels: 48.6 us -> 45.2 us
    pallas_call x1, Pallas kernels: 47.7 us -> 44.2 us  [on_device(): pl.pallas_call(functools.partial(kernel, n_seq, n_head), out_shape=(jax.S...]
where the time goes in v3:
time: 45.9 us
  Pallas kernels  45.2 us (98%)
  between operations  0.64 us (1%)
    pallas_call x1, Pallas kernels, on_device(): pl.pallas_call(functools.partial(kernel, n_seq, n_head), out_shape=(jax.S...  44.2 us
    pallas_call x1, Pallas kernels, on_device(): pl.pallas_call(store, out_shape=[jax.ShapeDtypeStruct(m.shape, m.dtype) f...  0.98 us

profile of v3, /device:TPU:120, one launch (start us, length us, event | category | flops | bytes accessed | tf_op | source)
XLA Modules:
  0.0 45.9 jit_solution(13624415872318796794)
XLA Ops:
  0.6 44.2 %shard_map.163 = (bf16[256,1024]{1,0:T(8,128)(2,1)S(1)}, f32[32,128]{1,0:T(8,128)S(1)}, f32[32,128]{1,0:T(8,128)S(1)}, bf16[256,512]{1,0:T(8,128)(2,1)S(1)}, bf1...) custom-call(bf16[256,1024]{1,0:T(8,128)(2,1)} %x_hbm.1, bf16[256,1024]{1,0:T(8,128)(2,1)} %g_hbm.1, ...), custom_call_target="tpu_custom_call" | custom-call | tf_op jit(solution)/shard_map/pallas_call | solution.py:610
  44.9 1.0 %shard_map.164 = (bf16[256,1024]{1,0:T(8,128)(2,1)}, f32[32,128]{1,0:T(8,128)}, f32[32,128]{1,0:T(8,128)}, bf16[256,512]{1,0:T(8,128)(2,1)}, bf16[256,128]{1,0:T(8,128)(2,1)}, /*index=5*/bf16[256,128]{1,0:T(8,128)(2,1)}) custom-call(bf16[256,1024]{1,0:T(8,128)(2,1)S(1)} %get-tuple-element.12.refs_0_, f32[32,128]{1,0:T(8,128)S(1)} %get-tuple-element.13.refs_1_, ...), custom_call_target="tpu_custom_call" | custom-call | tf_op jit(solution)/shard_map/pallas_call | solution.py:627

commit v4 on v3

--- a/solution.py
+++ b/solution.py
@@ -15,7 +15,6 @@
 SCALE = DIM ** (-0.5)
 SCALE2 = SCALE * math.log2(math.e)
 CHUNKS = 4
-ORDER = 0
 
 F32 = jnp.float32
 BF16 = jnp.bfloat16
@@ -369,7 +368,7 @@
             dp_all[o, :, head_lanes(i)] = nt(kv[o, 1], og_ref[:, cols(i)])
             return 0
 
-        lax.fori_loop(0, q_heads, one_head, 0)
+        lax.fori_loop(0, q_heads, one_head, 0, unroll=True)
 
     def softmax_step(i):
         here = head_lanes(i)
@@ -398,7 +397,7 @@
             dq_acc[i] += nn(kt[d], ds)
             return 0
 
-        lax.fori_loop(0, q_heads, one_head, 0)
+        lax.fori_loop(0, q_heads, one_head, 0, unroll=True)
 
     def kv_step(d):
         pl.when(exists(-d))(kv_copies[d].wait_recv)
@@ -406,22 +405,8 @@
 
     score_step(0)
     for d, c in zip((4, 1, 3, 2), range(CHUNKS)):
-        if ORDER == 0:
-            pair_step(c)
-            kv_step(d)
-        elif ORDER == 1:
-            kv_step(d)
-            pair_step(c)
-        elif ORDER == 2:
-            if c < 2:
-                pair_step(2 * c)
-                pair_step(2 * c + 1)
-            kv_step(d)
-        else:
-            kv_step(d)
-            if c >= 2:
-                pair_step(2 * c - 4)
-                pair_step(2 * c - 3)
+        pair_step(c)
+        kv_step(d)
 
     def attend_loop(c, _):
         softmax_step(c)

time: 45.9 us -> 44.8 us (0.976)
  Pallas kernels: 45.2 us -> 44.1 us
    pallas_call x1, Pallas kernels: 44.2 us -> 43.1 us  [on_device(): pl.pallas_call(functools.partial(kernel, n_seq, n_head), out_shape=(jax.S...]
where the time goes in v4:
time: 44.8 us; the launch traced here: 44.7 us
  Pallas kernels  44.1 us (98%)
  between operations  0.64 us (1%)
    pallas_call x1, Pallas kernels, on_device(): pl.pallas_call(functools.partial(kernel, n_seq, n_head), out_shape=(jax.S...  43.1 us
    pallas_call x1, Pallas kernels, on_device(): pl.pallas_call(store, out_shape=[jax.ShapeDtypeStruct(m.shape, m.dtype) f...  0.98 us

profile of v4, /device:TPU:120, one launch (start us, length us, event | category | flops | bytes accessed | tf_op | source)
XLA Modules:
  0.0 44.7 jit_solution(3110225685957206527)
XLA Ops:
  0.6 43.1 %shard_map.163 = (bf16[256,1024]{1,0:T(8,128)(2,1)S(1)}, f32[32,128]{1,0:T(8,128)S(1)}, f32[32,128]{1,0:T(8,128)S(1)}, bf16[256,512]{1,0:T(8,128)(2,1)S(1)}, bf1...) custom-call(bf16[256,1024]{1,0:T(8,128)(2,1)} %x_hbm.1, bf16[256,1024]{1,0:T(8,128)(2,1)} %g_hbm.1, ...), custom_call_target="tpu_custom_call" | custom-call | tf_op jit(solution)/shard_map/pallas_call | solution.py:595
  43.7 1.0 %shard_map.164 = (bf16[256,1024]{1,0:T(8,128)(2,1)}, f32[32,128]{1,0:T(8,128)}, f32[32,128]{1,0:T(8,128)}, bf16[256,512]{1,0:T(8,128)(2,1)}, bf16[256,128]{1,0:T(8,128)(2,1)}, /*index=5*/bf16[256,128]{1,0:T(8,128)(2,1)}) custom-call(bf16[256,1024]{1,0:T(8,128)(2,1)S(1)} %get-tuple-element.12.refs_0_, f32[32,128]{1,0:T(8,128)S(1)} %get-tuple-element.13.refs_1_, ...), custom_call_target="tpu_custom_call" | custom-call | tf_op jit(solution)/shard_map/pallas_call | solution.py:612

commit v5 on v4

--- a/solution.py
+++ b/solution.py
@@ -426,7 +426,7 @@
         )
 
     def grad_loop(step, _):
-        d = REACH - step
+        d = step + 1
         grad_step(d)
         dkv_out[d - 1, 0] = (nn(ds_all[d], q_rows[...]) * SCALE).astype(BF16)
         dkv_out[d - 1, 1] = nn(ph_all[d], og_rows[...]).astype(BF16)

time: 44.8 us -> 44 us (0.982)
  the two profiles are of different devices: /device:TPU:120 before, /device:TPU:105 now
where the time goes in v5:
time: 44 us; the launch traced here: 43.9 us
  Pallas kernels  43.3 us (98%)
  between operations  0.64 us (1%)
    pallas_call x1, Pallas kernels, on_device(): pl.pallas_call(functools.partial(kernel, n_seq, n_head), out_shape=(jax.S...  42.3 us
    pallas_call x1, Pallas kernels, on_device(): pl.pallas_call(store, out_shape=[jax.ShapeDtypeStruct(m.shape, m.dtype) f...  0.98 us

profile of v5, /device:TPU:105, one launch (start us, length us, event | category | flops | bytes accessed | tf_op | source)
XLA Modules:
  0.0 43.9 jit_solution(1477319041914465837)
XLA Ops:
  0.6 42.3 %shard_map.163 = (bf16[256,1024]{1,0:T(8,128)(2,1)S(1)}, f32[32,128]{1,0:T(8,128)S(1)}, f32[32,128]{1,0:T(8,128)S(1)}, bf16[256,512]{1,0:T(8,128)(2,1)S(1)}, bf1...) custom-call(bf16[256,1024]{1,0:T(8,128)(2,1)} %x_hbm.1, bf16[256,1024]{1,0:T(8,128)(2,1)} %g_hbm.1, ...), custom_call_target="tpu_custom_call" | custom-call | tf_op jit(solution)/shard_map/pallas_call | solution.py:595
  43.0 1.0 %shard_map.164 = (bf16[256,1024]{1,0:T(8,128)(2,1)}, f32[32,128]{1,0:T(8,128)}, f32[32,128]{1,0:T(8,128)}, bf16[256,512]{1,0:T(8,128)(2,1)}, bf16[256,128]{1,0:T(8,128)(2,1)}, /*index=5*/bf16[256,128]{1,0:T(8,128)(2,1)}) custom-call(bf16[256,1024]{1,0:T(8,128)(2,1)S(1)} %get-tuple-element.12.refs_0_, f32[32,128]{1,0:T(8,128)S(1)} %get-tuple-element.13.refs_1_, ...), custom_call_target="tpu_custom_call" | custom-call | tf_op jit(solution)/shard_map/pallas_call | solution.py:612
